TPU v7x, 128 devices: a whole 4x4x4 slice. The times are simulated.
128 devices in a mesh: dp: 32 (over z_lo, y, x), tensor: 4 (over z_hi, core).
Axes of the slice: x: 4, y: 4, z: 4 (z_hi: 2, z_lo: 2; z = z_hi * 2 + z_lo), core: 2. Of those that a mesh axis runs over, the one named last changes fastest.
Arguments:
- tokens: bfloat16 [16384, 1536], P(('dp', 'tensor')), may hold values from -6 to 6
- norm_gain: float32 [2, 2, 1536], replicated, may hold values from 0.1 to 1.9
- norm_shift: float32 [2, 2, 1536], replicated, may hold values from -3 to 3
- w_qkv: bfloat16 [2, 1536, 3, 1536], P(None, None, None, 'tensor'), may hold values from -0.15625 to 0.15625
- w_out: bfloat16 [2, 1536, 1536], P(None, 'tensor'), may hold values from -1.25 to 1.25
- w_up: bfloat16 [2, 1536, 6144], P(None, None, 'tensor'), may hold values from -0.15625 to 0.15625
- w_down: bfloat16 [2, 6144, 1536], P(None, 'tensor'), may hold values from -0.109375 to 0.109375
- granularity: int32 [32, 1], P('dp'), may hold values from 0 to 3
- cotangent: bfloat16 [16384, 1536], P(('dp', 'tensor')), may hold values from -24 to 24
Outputs:
- activations: bfloat16 [16384, 1536], P(('dp', 'tensor'))
- input_grad: float32 [16384, 1536], P(('dp', 'tensor'))
- grad_qkv: float32 [2, 1536, 3, 1536], P(None, 'dp', None, 'tensor')
- grad_out: float32 [2, 1536, 1536], P(None, 'tensor', 'dp')
- grad_up: float32 [2, 1536, 6144], P(None, 'dp', 'tensor')
- grad_down: float32 [2, 6144, 1536], P(None, 'tensor', 'dp')
- grad_gain: float32 [2, 2, 1536], replicated
- grad_shift: float32 [2, 2, 1536], replicated
- ffn_shift_grad: float32 [2, 1536], replicated
Inputs may be any that keep to these rules, and one draw needn't show every extreme that they name: Every granularity index 0, 1, 2 and 3 is given to some sequence.
All inputs are finite; a program needn't handle non-finite values.
Results may differ from a plain program's by a relative error of at most 0.035.
Values may be sent and summed in bfloat16 or wider, within the bound.
No kernel may reach another device: no remote copies, remote signals or barrier semaphores. Data moves between devices by JAX's collectives and lax.ppermute only.
A program may use at most 192 MiB of HBM per device.

v0:
```python
import jax
import jax.numpy as jnp
from jax import lax
from jax.sharding import PartitionSpec as P

HEAD_SIZE = 128
FF = 6144


norm_epsilon = 1e-05
rotary_base = 10000.0
masked_score = -1e30


def layer_norm(values, gain_row, shift_row):
    centered = values - jnp.mean(values, axis=-1, keepdims=True)
    variance = jnp.mean(centered * centered, axis=-1, keepdims=True)
    return centered * lax.rsqrt(variance + norm_epsilon) * gain_row + shift_row


def rotary_tables(length, head_size):
    half_size = head_size // 2
    places = jnp.arange(length, dtype=jnp.float32)[:, None]
    frequency = rotary_base ** (-jnp.arange(half_size, dtype=jnp.float32) / half_size)
    angles = places * frequency[None, :]
    return (jnp.cos(angles)[:, None, :], jnp.sin(angles)[:, None, :])


def rotate(values, cosine_table, sine_table):
    half_size = values.shape[-1] // 2
    first_half = values[..., :half_size]
    second_half = values[..., half_size:]
    return jnp.concatenate(
        [
            first_half * cosine_table - second_half * sine_table,
            second_half * cosine_table + first_half * sine_table,
        ],
        axis=-1,
    )


def body(tokens, norm_gain, norm_shift, w_qkv, w_out, w_up, w_down, granularity, cotangent):
    tensor_count = lax.axis_size("tensor")
    tensor_place = lax.axis_index("tensor")
    local_rows = tokens.shape[0]
    length = local_rows * tensor_count
    layers = w_qkv.shape[0]
    head_size = HEAD_SIZE
    local_width = w_qkv.shape[3]
    local_heads = local_width // head_size
    slice_width = w_up.shape[2]
    prefix_width = FF // 8 * 2 ** granularity[0, 0]
    columns = tensor_place * slice_width + jnp.arange(slice_width, dtype=jnp.int32)
    keep_mask = (columns < prefix_width).astype(jnp.float32)
    block_rows = min(512, length)
    blocks = length // block_rows
    cosine_table, sine_table = rotary_tables(length, head_size)
    query_scale = head_size ** (-0.5)
    head_shape = (length, local_heads, head_size)
    block_shape = (blocks, block_rows, local_heads, head_size)
    starts = jnp.arange(blocks, dtype=jnp.int32) * block_rows
    key_places = jnp.arange(length, dtype=jnp.int32)

    def gather_rows(values):
        return lax.all_gather(values, "tensor", axis=0, tiled=True)

    def sum_rows(term):
        return lax.psum_scatter(
            term(jnp.int32(0), lax.axis_size("tensor") * local_rows).astype(jnp.bfloat16),
            "tensor",
            scatter_dimension=0,
            tiled=True,
        ).astype(jnp.float32)

    def gather_gradients(values):
        return lax.all_gather(values, "tensor", axis=0, tiled=True)

    def sum_gradients(term):
        return lax.psum_scatter(
            term(jnp.int32(0), lax.axis_size("tensor") * local_rows).astype(jnp.bfloat16),
            "tensor",
            scatter_dimension=0,
            tiled=True,
        ).astype(jnp.float32)

    def activate(values):
        return jax.nn.gelu(values, approximate=True) * keep_mask

    def turn_query(values):
        return rotate(values, cosine_table, sine_table) * query_scale

    def turn_key(values):
        return rotate(values, cosine_table, sine_table)

    def block_scores(query_block, key_rows, row_start):
        places = row_start + jnp.arange(block_rows, dtype=jnp.int32)
        allowed = key_places[None, :] <= places[:, None]
        scores = jnp.einsum(
            "qhe,khe->hqk", query_block, key_rows, preferred_element_type=jnp.float32
        )
        return jnp.where(allowed[None], scores, masked_score)

    def attend_back(queries, key_rows, value_rows, log_total, mixture_gradient):

        def one_block(totals, entries):
            key_gradient, value_gradient = totals
            query_block, row_start, log_block, gradient_block = entries
            scores = block_scores(query_block, key_rows, row_start)
            probability = jnp.exp(scores - log_block)
            probability_low = probability.astype(jnp.bfloat16)
            value_gradient = value_gradient + jnp.einsum(
                "hqk,qhe->khe", probability_low, gradient_block, preferred_element_type=jnp.float32
            )
            weight_gradient = jnp.einsum(
                "qhe,khe->hqk", gradient_block, value_rows, preferred_element_type=jnp.float32
            )
            row_inner = jnp.sum(probability * weight_gradient, axis=-1, keepdims=True)
            score_gradient = (probability * (weight_gradient - row_inner)).astype(jnp.bfloat16)
            query_gradient = jnp.einsum(
                "hqk,khe->qhe", score_gradient, key_rows, preferred_element_type=jnp.float32
            )
            key_gradient = key_gradient + jnp.einsum(
                "hqk,qhe->khe", score_gradient, query_block, preferred_element_type=jnp.float32
            )
            return ((key_gradient, value_gradient), query_gradient)

        zero_rows = jnp.zeros(head_shape, jnp.float32)
        (key_gradient, value_gradient), query_gradient = lax.scan(
            one_block,
            (zero_rows, zero_rows),
            (
                queries.reshape(block_shape),
                starts,
                log_total,
                mixture_gradient.reshape(block_shape),
            ),
        )
        return (query_gradient.reshape(head_shape), key_gradient, value_gradient)

    def layer_back(layer_index, out_gradient, saved_layer):
        feed_gradient = gather_gradients(out_gradient.astype(jnp.bfloat16))
        up_weight = w_up[layer_index]
        down_weight = w_down[layer_index]
        down_gradient = jnp.einsum(
            "tf,td->fd", saved_layer["hidden"], feed_gradient, preferred_element_type=jnp.float32
        )
        hidden_gradient = jnp.einsum(
            "td,fd->tf", feed_gradient, down_weight, preferred_element_type=jnp.float32
        )
        feed_upward_gradient = jax.vjp(activate, saved_layer["upward"])[1](hidden_gradient)[
            0
        ].astype(jnp.bfloat16)
        up_gradient = jnp.einsum(
            "td,tf->df",
            saved_layer["gathered two"],
            feed_upward_gradient,
            preferred_element_type=jnp.float32,
        )
        down_gradient, up_gradient, upward_gradient = (
            down_gradient,
            up_gradient,
            feed_upward_gradient,
        )

        def normed_two_term(row_start, row_count):
            return (
                jnp.einsum(
                    "tf,df->td", upward_gradient, up_weight, preferred_element_type=jnp.float32
                ),
            )[0]

        normed_two_gradient = sum_gradients(normed_two_term)
        middle_part, gain_two, shift_two = saved_layer["norm back two"](normed_two_gradient)
        middle_gradient = out_gradient + middle_part
        attention_gradient = gather_gradients(middle_gradient.astype(jnp.bfloat16))
        out_weight_gradient = jnp.einsum(
            "th,td->hd",
            saved_layer["mixture"],
            attention_gradient,
            preferred_element_type=jnp.float32,
        )
        mixture_gradient = jnp.einsum(
            "td,hd->th", attention_gradient, w_out[layer_index], preferred_element_type=jnp.float32
        ).astype(jnp.bfloat16)
        query_gradient, key_gradient, value_gradient = attend_back(
            saved_layer["queries"],
            saved_layer["key rows"],
            saved_layer["value rows"],
            saved_layer["log total"],
            mixture_gradient,
        )
        query_gradient = (
            saved_layer["query back"](query_gradient)[0]
            .reshape(length, local_width)
            .astype(jnp.bfloat16)
        )
        key_gradient = (
            saved_layer["key back"](key_gradient)[0]
            .reshape(length, local_width)
            .astype(jnp.bfloat16)
        )
        value_gradient = value_gradient.reshape(length, local_width).astype(jnp.bfloat16)
        projected_gradient = jnp.stack([query_gradient, key_gradient, value_gradient], axis=1)
        qkv_gradient = jnp.einsum(
            "td,tch->dch",
            saved_layer["gathered"],
            projected_gradient,
            preferred_element_type=jnp.float32,
        )
        qkv_weight = w_qkv[layer_index]

        def normed_term(row_start, row_count):
            return jnp.einsum(
                "tch,dch->td", projected_gradient, qkv_weight, preferred_element_type=jnp.float32
            )

        normed_gradient = sum_gradients(normed_term)
        stream_part, gain_one, shift_one = saved_layer["norm back"](normed_gradient)
        stream_gradient = middle_gradient + stream_part
        weight_gradients = (qkv_gradient, out_weight_gradient, up_gradient, down_gradient)
        return (
            stream_gradient,
            weight_gradients,
            (jnp.stack([gain_one, gain_two]), jnp.stack([shift_one, shift_two])),
        )

    stream = tokens.astype(jnp.float32)
    saved_list = []
    for layer_index in range(layers):
        normed, norm_back = jax.vjp(
            layer_norm, stream, norm_gain[layer_index, 0], norm_shift[layer_index, 0]
        )
        gathered = gather_rows(normed.astype(jnp.bfloat16))
        projected = jnp.einsum(
            "td,dch->tch", gathered, w_qkv[layer_index], preferred_element_type=jnp.float32
        )
        layer_queries, query_back = jax.vjp(turn_query, projected[:, 0].reshape(head_shape))
        layer_key_rows, key_back = jax.vjp(turn_key, projected[:, 1].reshape(head_shape))
        layer_queries = layer_queries.astype(jnp.bfloat16)
        layer_key_rows = layer_key_rows.astype(jnp.bfloat16)
        layer_value_rows = projected[:, 2].reshape(head_shape).astype(jnp.bfloat16)
        attend_key_rows = layer_key_rows
        attend_value_rows = layer_value_rows

        def attend_one_block(entries):
            query_block, row_start = entries
            scores = block_scores(query_block, attend_key_rows, row_start)
            row_top = jnp.max(scores, axis=-1, keepdims=True)
            exponent = jnp.exp(scores - row_top)
            row_total = jnp.sum(exponent, axis=-1, keepdims=True)
            weights_low = (exponent / row_total).astype(jnp.bfloat16)
            mixture = jnp.einsum(
                "hqk,khe->qhe", weights_low, attend_value_rows, preferred_element_type=jnp.float32
            )
            return (mixture, row_top + jnp.log(row_total))

        mixture, attend_log_total = lax.map(
            attend_one_block, (layer_queries.reshape(block_shape), starts)
        )
        layer_mixture = mixture.reshape(length, local_width).astype(jnp.bfloat16)
        out_weight = w_out[layer_index]

        def attention_term(row_start, row_count):
            return jnp.dot(layer_mixture, out_weight, preferred_element_type=jnp.float32)

        middle = stream + sum_rows(attention_term)
        normed_two, norm_back_two = jax.vjp(
            layer_norm, middle, norm_gain[layer_index, 1], norm_shift[layer_index, 1]
        )
        gathered_two = gather_rows(normed_two.astype(jnp.bfloat16))
        layer_up_weight = w_up[layer_index]
        layer_down_weight = w_down[layer_index]
        upward = jnp.dot(gathered_two, layer_up_weight, preferred_element_type=jnp.float32)
        upward, hidden = (upward, activate(upward).astype(jnp.bfloat16))

        def feed_term(row_start, row_count):
            return (jnp.dot(hidden, layer_down_weight, preferred_element_type=jnp.float32),)[0]

        result = middle + sum_rows(feed_term)
        layer_saved_layer = {
            "norm back": norm_back,
            "gathered": gathered,
            "query back": query_back,
            "key back": key_back,
            "queries": layer_queries,
            "key rows": layer_key_rows,
            "value rows": layer_value_rows,
            "mixture": layer_mixture,
            "log total": attend_log_total,
            "norm back two": norm_back_two,
            "gathered two": gathered_two,
            "upward": upward,
            "hidden": hidden,
        }
        stream = result
        saved_layer = layer_saved_layer
        saved_list.append(saved_layer)
    activations = stream.astype(jnp.bfloat16)
    gradient = cotangent.astype(jnp.float32)
    weight_list = [None] * layers
    norm_list = [None] * layers
    for layer_index in reversed(range(layers)):
        gradient, weight_gradients, norm_gradients = layer_back(
            layer_index, gradient, saved_list[layer_index]
        )
        weight_list[layer_index] = weight_gradients
        norm_list[layer_index] = norm_gradients
    stacked = tuple(
        (
            jnp.stack([weight_list[layer_index][member] for layer_index in range(layers)])
            for member in range(4)
        )
    )
    stacked = (
        lax.psum_scatter(
            stacked[0].astype(jnp.bfloat16), "dp", scatter_dimension=1, tiled=True
        ).astype(jnp.float32),
        lax.psum_scatter(
            stacked[1].astype(jnp.bfloat16), "dp", scatter_dimension=2, tiled=True
        ).astype(jnp.float32),
        lax.psum_scatter(
            stacked[2].astype(jnp.bfloat16), "dp", scatter_dimension=1, tiled=True
        ).astype(jnp.float32),
        lax.psum_scatter(
            stacked[3].astype(jnp.bfloat16), "dp", scatter_dimension=2, tiled=True
        ).astype(jnp.float32),
    )
    gain_grads = jnp.stack([norm_list[layer_index][0] for layer_index in range(layers)])
    shift_grads = jnp.stack([norm_list[layer_index][1] for layer_index in range(layers)])
    gain_grads, shift_grads = lax.psum((gain_grads, shift_grads), ("dp", "tensor"))
    ffn_shift_grad = shift_grads[:, 1, :]
    return (
        activations,
        gradient,
        stacked[0],
        stacked[1],
        stacked[2],
        stacked[3],
        gain_grads,
        shift_grads,
        ffn_shift_grad,
    )


def solution(mesh):
    return jax.shard_map(
        body,
        mesh=mesh,
        in_specs=(
            P(("dp", "tensor"), None),
            P(),
            P(),
            P(None, None, None, "tensor"),
            P(None, "tensor", None),
            P(None, None, "tensor"),
            P(None, "tensor", None),
            P("dp", None),
            P(("dp", "tensor"), None),
        ),
        out_specs=(
            P(("dp", "tensor"), None),
            P(("dp", "tensor"), None),
            P(None, "dp", None, "tensor"),
            P(None, "tensor", "dp"),
            P(None, "dp", "tensor"),
            P(None, "tensor", "dp"),
            P(),
            P(),
            P(),
        ),
        check_vma=False,
    )
```

profile of v0, /device:TPU:10, one launch (start us, length us, event | category | flops | bytes accessed | tf_op | source)
XLA Modules:
  0.0 1388.0 jit_solution(9995400548405635868)
XLA Ops:
  15.8 25.1 %all-gather.9.cloned.1.call-done = bf16[512,1536]{1,0:T(8,128)(2,1)} async-done(((bf16[128,1536]{1,0:T(8,128)(2,1)}), bf16[512,1536]{1,0:T(8,128)(2,1)}) %all-gather.9.cloned.1.call-update) | async-done | bytes 1572880 | tf_op jit(solution)/shard_map/all_gather | solution.py:65
  58.3 34.5 %reduce-scatter.11.cloned.1.call-done = bf16[128,1536]{1,0:T(8,128)(2,1)} async-done(((bf16[512,1536]{1,0:T(8,128)(2,1)}), bf16[128,1536]{1,0:T(8,128)(2,1)}) %reduce-scatter.11.cloned.1.call-update) | async-done | bytes 393232 | tf_op jit(solution)/shard_map/reduce_scatter | solution.py:68
  99.8 21.7 %all-gather.11.cloned.1.call-done = bf16[512,1536]{1,0:T(8,128)(2,1)} async-done(((bf16[128,1536]{1,0:T(8,128)(2,1)}), bf16[512,1536]{1,0:T(8,128)(2,1)}) %all-gather.11.cloned.1.call-update) | async-done | bytes 1572880 | tf_op jit(solution)/shard_map/all_gather | solution.py:65
  134.6 34.5 %reduce-scatter.13.cloned.1.call-done = bf16[128,1536]{1,0:T(8,128)(2,1)} async-done(((bf16[512,1536]{1,0:T(8,128)(2,1)}), bf16[128,1536]{1,0:T(8,128)(2,1)}) %reduce-scatter.13.cloned.1.call-update) | async-done | bytes 393232 | tf_op jit(solution)/shard_map/reduce_scatter | solution.py:68
  173.6 23.1 %all-gather.13.cloned.1.call-done = bf16[512,1536]{1,0:T(8,128)(2,1)} async-done(((bf16[128,1536]{1,0:T(8,128)(2,1)}), bf16[512,1536]{1,0:T(8,128)(2,1)}) %all-gather.13.cloned.1.call-update) | async-done | bytes 1572880 | tf_op jit(solution)/shard_map/all_gather | solution.py:65
  223.5 34.5 %reduce-scatter.15.cloned.1.call-done = bf16[128,1536]{1,0:T(8,128)(2,1)} async-done(((bf16[512,1536]{1,0:T(8,128)(2,1)}), bf16[128,1536]{1,0:T(8,128)(2,1)}) %reduce-scatter.15.cloned.1.call-update) | async-done | bytes 393232 | tf_op jit(solution)/shard_map/reduce_scatter | solution.py:68
  263.4 22.2 %all-gather.15.cloned.1.call-done = bf16[512,1536]{1,0:T(8,128)(2,1)} async-done(((bf16[128,1536]{1,0:T(8,128)(2,1)}), bf16[512,1536]{1,0:T(8,128)(2,1)}) %all-gather.15.cloned.1.call-update) | async-done | bytes 1572880 | tf_op jit(solution)/shard_map/all_gather | solution.py:65
  292.7 17.7 %all-gather.17.cloned.1.call-done = bf16[512,1536]{1,0:T(8,128)(2,1)} async-done(((bf16[128,1536]{1,0:T(8,128)(2,1)}), bf16[512,1536]{1,0:T(8,128)(2,1)}) %all-gather.17.cloned.1.call-update) | async-done | bytes 1572880 | tf_op jit(solution)/shard_map/all_gather | solution.py:76
  310.4 8.0 fusion.63
  333.2 27.1 %reduce-scatter.19.cloned.1.call-done = bf16[128,1536]{1,0:T(8,128)(2,1)} async-done(((bf16[512,1536]{1,0:T(8,128)(2,1)}), bf16[128,1536]{1,0:T(8,128)(2,1)}) %reduce-scatter.19.cloned.1.call-update) | async-done | bytes 393232 | tf_op jit(solution)/shard_map/reduce_scatter | solution.py:79
  363.5 33.7 %reduce-scatter.17.cloned.1.call-done = bf16[128,1536]{1,0:T(8,128)(2,1)} async-done(((bf16[512,1536]{1,0:T(8,128)(2,1)}), bf16[128,1536]{1,0:T(8,128)(2,1)}) %reduce-scatter.17.cloned.1.call-update) | async-done | bytes 393232 | tf_op jit(solution)/shard_map/reduce_scatter | solution.py:68
  404.1 21.6 %all-gather.19.cloned.1.call-done = bf16[512,1536]{1,0:T(8,128)(2,1)} async-done(((bf16[128,1536]{1,0:T(8,128)(2,1)}), bf16[512,1536]{1,0:T(8,128)(2,1)}) %all-gather.19.cloned.1.call-update) | async-done | bytes 1572880 | tf_op jit(solution)/shard_map/all_gather | solution.py:76
  455.0 34.5 %reduce-scatter.21.cloned.1.call-done = bf16[128,1536]{1,0:T(8,128)(2,1)} async-done(((bf16[512,1536]{1,0:T(8,128)(2,1)}), bf16[128,1536]{1,0:T(8,128)(2,1)}) %reduce-scatter.21.cloned.1.call-update) | async-done | bytes 393232 | tf_op jit(solution)/shard_map/reduce_scatter | solution.py:79
  498.1 22.7 %all-gather.21.cloned.1.call-done = bf16[512,1536]{1,0:T(8,128)(2,1)} async-done(((bf16[128,1536]{1,0:T(8,128)(2,1)}), bf16[512,1536]{1,0:T(8,128)(2,1)}) %all-gather.21.cloned.1.call-update) | async-done | bytes 1572880 | tf_op jit(solution)/shard_map/all_gather | solution.py:76
  520.8 8.0 fusion.56
  536.1 34.5 %reduce-scatter.23.cloned.1.call-done = bf16[128,1536]{1,0:T(8,128)(2,1)} async-done(((bf16[512,1536]{1,0:T(8,128)(2,1)}), bf16[128,1536]{1,0:T(8,128)(2,1)}) %reduce-scatter.23.cloned.1.call-update) | async-done | bytes 393232 | tf_op jit(solution)/shard_map/reduce_scatter | solution.py:79
  580.0 21.7 %all-gather.23.cloned.1.call-done = bf16[512,1536]{1,0:T(8,128)(2,1)} async-done(((bf16[128,1536]{1,0:T(8,128)(2,1)}), bf16[512,1536]{1,0:T(8,128)(2,1)}) %all-gather.23.cloned.1.call-update) | async-done | bytes 1572880 | tf_op jit(solution)/shard_map/all_gather | solution.py:76
  634.2 8.3 pad_maximum_fusion.1
  642.5 24.1 %copy.145 = bf16[2,1536,1536]{1,0,2:T(2,128)(2,1)} copy(bf16[2,1536,1536]{2,1,0:T(8,128)(2,1)} %pad_maximum_fusion.1) | data formatting | bytes 18874368 | tf_op jit(solution)/shard_map/stack | solution.py:310
  684.0 8.4 pad_maximum_fusion
  708.4 68.2 %all-reduce.10 = (f32[2,2,1536]{2,1,0:T(2,128)}, f32[2,2,1536]{2,1,0:T(2,128)S(1)}) all-reduce(f32[2,2,1536]{2,1,0:T(2,128)S(1)} %pad_maximum_fusion.16, f32[2,2,1536]{2,1,0:T(2,128)S(1)} %pad_maximum_fusion.17), channel_id=1, replica_groups=mesh['dp'=32,'tensor'=4] {'dp','tensor'}, use_global_device_ids=true, to_apply=%region_38.39 | all-reduce | flops 12288 | bytes 98304 | tf_op jit(solution)/shard_map/psum | solution.py:330
  779.7 245.9 %all-reduce.14.cloned.1.call-done = (bf16[2,384,1536]{1,0,2:T(2,128)(2,1)}, bf16[2,1536,1536]{1,0,2:T(2,128)(2,1)}) async-done(((bf16[2,384,1536]{1,0,2:T(2,128)(2,1)}, bf16[2,1536,1536]{1,0,2:T(2,128)(2,1)}), (bf16[2,384,1536]{1,0,2:T(2,128)(2,1)}, bf16[2,1536,1536]{1,0,2:T(2,128)(2,1)})) %all-reduce.14.cloned.1.call-update) | async-done | bytes 11796496
  1029.3 174.7 %reduce-scatter.29.cloned.1.call-done = bf16[2,48,1536]{2,1,0:T(8,128)(2,1)} async-done(((bf16[2,1536,1536]{2,1,0:T(8,128)(2,1)}), bf16[2,48,1536]{2,1,0:T(8,128)(2,1)}) %reduce-scatter.29.cloned.1.call-update) | async-done | bytes 294928 | tf_op jit(solution)/shard_map/reduce_scatter | solution.py:321
  1205.8 173.5 %reduce-scatter.27.cloned.1.call-done = bf16[2,48,3,384]{3,1,2,0:T(8,128)(2,1)} async-done(((bf16[2,1536,3,384]{3,1,2,0:T(8,128)(2,1)}), bf16[2,48,3,384]{3,1,2,0:T(8,128)(2,1)}) %reduce-scatter.27.cloned.1.call-update) | async-done | bytes 221200 | tf_op jit(solution)/shard_map/reduce_scatter | solution.py:315
  (386 shorter events, 242.9 us)
Async XLA Ops:
  7.2 33.7 %all-gather.9.cloned.1.call-start = ((), (), s32[]{:S(2)}) async-start(), calls=%async_computation.10 | async-start | bytes 1966080 | tf_op jit(solution)/shard_map/all_gather | solution.py:65
  14.6 78.1 %reduce-scatter.11.cloned.1.call-start = ((), (), s32[]{:S(2)}) async-start(), calls=%async_computation.11 | async-start | bytes 1966080 | tf_op jit(solution)/shard_map/reduce_scatter | solution.py:68
  58.2 63.3 %all-gather.11.cloned.1.call-start = ((), (), s32[]{:S(2)}) async-start(), calls=%async_computation.12 | async-start | bytes 1966080 | tf_op jit(solution)/shard_map/all_gather | solution.py:65
  98.3 70.9 %reduce-scatter.13.cloned.1.call-start = ((), (), s32[]{:S(2)}) async-start(), calls=%async_computation.13 | async-start | bytes 1966080 | tf_op jit(solution)/shard_map/reduce_scatter | solution.py:68
  134.6 62.2 %all-gather.13.cloned.1.call-start = ((), (), s32[]{:S(2)}) async-start(), calls=%async_computation.14 | async-start | bytes 1966080 | tf_op jit(solution)/shard_map/all_gather | solution.py:65
  173.6 84.5 %reduce-scatter.15.cloned.1.call-start = ((), (), s32[]{:S(2)}) async-start(), calls=%async_computation.15 | async-start | bytes 1966080 | tf_op jit(solution)/shard_map/reduce_scatter | solution.py:68
  223.5 62.1 %all-gather.15.cloned.1.call-start = ((), (), s32[]{:S(2)}) async-start(), calls=%async_computation.16 | async-start | bytes 1966080 | tf_op jit(solution)/shard_map/all_gather | solution.py:65
  262.4 48.0 %all-gather.17.cloned.1.call-start = ((), (), s32[]{:S(2)}) async-start(), calls=%async_computation.18 | async-start | bytes 1966080 | tf_op jit(solution)/shard_map/all_gather | solution.py:76
  263.1 97.1 %reduce-scatter.19.cloned.1.call-start = ((), (), s32[]{:S(2)}) async-start(), calls=%async_computation.19 | async-start | bytes 1966080 | tf_op jit(solution)/shard_map/reduce_scatter | solution.py:79
  325.7 71.5 %reduce-scatter.17.cloned.1.call-start = ((), (), s32[]{:S(2)}) async-start(), calls=%async_computation.17 | async-start | bytes 1966080 | tf_op jit(solution)/shard_map/reduce_scatter | solution.py:68
  333.1 92.6 %all-gather.19.cloned.1.call-start = ((), (), s32[]{:S(2)}) async-start(), calls=%async_computation.20 | async-start | bytes 1966080 | tf_op jit(solution)/shard_map/all_gather | solution.py:76
  402.5 87.0 %reduce-scatter.21.cloned.1.call-start = ((), (), s32[]{:S(2)}) async-start(), calls=%async_computation.21 | async-start | bytes 1966080 | tf_op jit(solution)/shard_map/reduce_scatter | solution.py:79
  454.9 65.9 %all-gather.21.cloned.1.call-start = ((), (), s32[]{:S(2)}) async-start(), calls=%async_computation.22 | async-start | bytes 1966080 | tf_op jit(solution)/shard_map/all_gather | solution.py:76
  497.6 73.0 %reduce-scatter.23.cloned.1.call-start = ((), (), s32[]{:S(2)}) async-start(), calls=%async_computation.23 | async-start | bytes 1966080 | tf_op jit(solution)/shard_map/reduce_scatter | solution.py:79
  536.0 65.7 %all-gather.23.cloned.1.call-start = ((), (), s32[]{:S(2)}) async-start(), calls=%async_computation.24 | async-start | bytes 1966080 | tf_op jit(solution)/shard_map/all_gather | solution.py:76
  578.5 127.0 %reduce-scatter.25.cloned.1.call-start = ((), (), s32[]{:S(2)}) async-start(), calls=%async_computation.25 | async-start | bytes 1966080 | tf_op jit(solution)/shard_map/reduce_scatter | solution.py:79
  619.5 406.1 %all-reduce.14.cloned.1.call-start = ((), (), s32[]{:S(2)}) async-start(), calls=%async_computation.28 | async-start | bytes 23592960
  672.8 531.2 %reduce-scatter.29.cloned.1.call-start = ((), (), s32[]{:S(2)}) async-start(), calls=%async_computation.27 | async-start | bytes 9732096 | tf_op jit(solution)/shard_map/reduce_scatter | solution.py:321
  692.4 686.9 %reduce-scatter.27.cloned.1.call-start = ((), (), s32[]{:S(2)}) async-start(), calls=%async_computation.26 | async-start | bytes 7299072 | tf_op jit(solution)/shard_map/reduce_scatter | solution.py:315
  703.5 73.7 %copy-start.4 = (bf16[128,1536]{1,0:T(8,128)(2,1)S(1)}, bf16[128,1536]{1,0:T(8,128)(2,1)}, u32[]{:S(2)}) copy-start(bf16[128,1536]{1,0:T(8,128)(2,1)} %reduce-scatter.11.cloned.1.call-done) | copy-start | bytes 1179652
  703.5 73.7 %copy-start.11 = (f32[128,1536]{1,0:T(8,128)S(1)}, f32[128,1536]{1,0:T(8,128)}, u32[]{:S(2)}) copy-start(f32[128,1536]{1,0:T(8,128)} %get-tuple-element.166) | copy-start | bytes 2359300
  703.5 73.7 %copy-start.16 = (bf16[128,1536]{1,0:T(8,128)(2,1)S(1)}, bf16[128,1536]{1,0:T(8,128)(2,1)}, u32[]{:S(2)}) copy-start(bf16[128,1536]{1,0:T(8,128)(2,1)} %reduce-scatter.23.cloned.1.call-done) | copy-start | bytes 1179652
  703.5 73.7 %copy-start.59 = (f32[128]{0:T(128)S(1)}, f32[128]{0:T(128)}, u32[]{:S(2)}) copy-start(f32[128]{0:T(128)} %copy-done.58) | copy-start | bytes 1540
  776.6 429.3 %copy-start.68 = (f32[2,2,1536]{2,1,0:T(2,128)}, f32[2,2,1536]{2,1,0:T(2,128)S(1)}, u32[]{:S(2)}) copy-start(f32[2,2,1536]{2,1,0:T(2,128)S(1)} %get-tuple-element.162) | copy-start | bytes 73732
  (95 other events, 668.4 us)
Sparse Core Ops, SparseCore 0:
  14.8 26.1 all-gather.8
  58.3 34.3 reduce-scatter.10
  98.4 23.0 all-gather.10
  134.7 34.4 reduce-scatter.12
  173.7 23.0 all-gather.12
  223.6 34.3 reduce-scatter.14
  262.5 23.0 all-gather.14
  287.4 23.0 all-gather.16
  325.8 34.4 reduce-scatter.18
  362.7 34.4 reduce-scatter.16
  402.6 23.0 all-gather.18
  455.0 34.4 reduce-scatter.20
  497.7 23.0 all-gather.20
  536.1 34.3 reduce-scatter.22
  578.6 23.0 all-gather.22
  619.6 34.4 reduce-scatter.24
  672.9 352.6 all-reduce.13
  1028.0 175.9 reduce-scatter.28
  1206.6 172.7 reduce-scatter.26
where the time goes:
time: 1410 us; the launch traced here: 1390 us
  waiting for transfers between devices  1000 us (71%)
  matrix products  130 us (9%)
  other arithmetic  87.6 us (6%)
  local copies, waits for them, and re-layouts  78.1 us (6%)
  blocking collectives  68.2 us (5%)
  between operations  17.1 us (1%)
    unnamed x20, waiting for transfers between devices  247 us
    reduce_scatter x1, waiting for transfers between devices, body(): lax.psum_scatter(stacked[2].astype(jnp.bfloat16), 'dp', scatter_dimension...  175 us
    reduce_scatter x1, waiting for transfers between devices, body(): lax.psum_scatter(stacked[0].astype(jnp.bfloat16), 'dp', scatter_dimension...  173 us
    reduce_scatter x4, waiting for transfers between devices, sum_rows(): lax.psum_scatter(term(jnp.int32(0), lax.axis_size('tensor') * local_rows)...  137 us
    reduce_scatter x4, waiting for transfers between devices, sum_gradients(): lax.psum_scatter(term(jnp.int32(0), lax.axis_size('tensor') * local_rows)...  96.2 us
    all_gather x4, waiting for transfers between devices, gather_rows(): return lax.all_gather(values, 'tensor', axis=0, tiled=True)  92.1 us
    all_gather x4, waiting for transfers between devices, gather_gradients(): return lax.all_gather(values, 'tensor', axis=0, tiled=True)  83.6 us
    psum x1, blocking collectives, body(): lax.psum((gain_grads, shift_grads), ('dp', 'tensor'))  68.2 us
  transfers between devices with their start and end apart: 19, of which 18 were waited for; matrix products, arithmetic and copies ran while one was open for 8% of the time, Pallas kernels for 0%

commit v1 on v0

v1 whole, which is shorter than its diff:
```python
import functools
import itertools

import jax
import jax.numpy as jnp
from jax import lax
from jax.experimental import pallas as pl
from jax.experimental.pallas import tpu as pltpu
from jax.sharding import Mesh
from jax.sharding import PartitionSpec as P

D = 1536
FF = 6144
E = 128
HEADS = 3
HID = HEADS * E
SLICE = 1536
HALF = 256
OWN = 128
FB = 384
EPS = 1e-5
BASE = 10000.0
MASKED = -1e30
SCALE = E**-0.5
C1 = 0.7978845608028654
C2 = 0.044715

AXES = ("zl", "y", "x", "zh", "c")
SIZES = (2, 4, 4, 2, 2)
F32 = jnp.float32
BF16 = jnp.bfloat16


def flat(place):
    index = 0
    for size, at in zip(SIZES, place):
        index = index * size + at
    return index


def pairs(move):
    return [
        (flat(p), flat(move(*p))) for p in itertools.product(*[range(s) for s in SIZES])
    ]


CORE = pairs(lambda zl, y, x, zh, c: (zl, y, x, zh, 1 - c))
FAR = pairs(lambda zl, y, x, zh, c: (zl, y, x, 1 - zh, c))
ZLO = pairs(lambda zl, y, x, zh, c: (1 - zl, y, x, zh, c))


def x_by(d):
    return pairs(lambda zl, y, x, zh, c: (zl, y, (x + d) % 4, zh, c))


def y_by(d):
    return pairs(lambda zl, y, x, zh, c: (zl, (y + d) % 4, x, zh, c))


def x_flip(d):
    return pairs(lambda zl, y, x, zh, c: (zl, y, x ^ d, zh, c))


def y_flip(d):
    return pairs(lambda zl, y, x, zh, c: (zl, y ^ d, x, zh, c))


def send(values, perm):
    return lax.ppermute(values, AXES, perm)


def dot(a, b):
    return jnp.dot(a, b, preferred_element_type=F32)


def dot_t(a, b):
    return lax.dot_general(a, b, (((1,), (1,)), ((), ())), preferred_element_type=F32)


def t_dot(a, b):
    return lax.dot_general(a, b, (((0,), (0,)), ((), ())), preferred_element_type=F32)


def params(mb):
    return pltpu.CompilerParams(vmem_limit_bytes=mb * 1024 * 1024)


def cost(flops, size, trans=0):
    return pl.CostEstimate(flops=int(flops), bytes_accessed=int(size), transcendentals=int(trans))


def whole(shape):
    zeros = (0,) * len(shape)
    return pl.BlockSpec(shape, lambda *_: zeros)


SMEM = pl.BlockSpec(memory_space=pltpu.SMEM)


def moments(x):
    mean = jnp.mean(x, axis=-1, keepdims=True)
    centered = x - mean
    var = jnp.mean(centered * centered, axis=-1, keepdims=True)
    return centered, lax.rsqrt(var + EPS)


def norm_kernel(x_ref, g_ref, b_ref, a_ref):
    centered, r = moments(x_ref[...].astype(F32))
    a_ref[...] = (centered * r * g_ref[...] + b_ref[...]).astype(BF16)


def norm(x, gain, shift):
    rows = x.shape[0]
    return pl.pallas_call(
        norm_kernel,
        out_shape=jax.ShapeDtypeStruct((rows, D), BF16),
        in_specs=[whole((rows, D)), whole((1, D)), whole((1, D))],
        out_specs=whole((rows, D)),
        grid=(1,),
        compiler_params=params(16),
        cost_estimate=cost(10 * rows * D, 6 * rows * D),
        name="norm",
    )(x, gain, shift)


def add_norm_kernel(x_ref, s_ref, r_ref, g_ref, b_ref, m_ref, a_ref):
    x = x_ref[...].astype(F32) + (s_ref[...].astype(F32) + r_ref[...].astype(F32))
    m_ref[...] = x
    centered, r = moments(x)
    a_ref[...] = (centered * r * g_ref[...] + b_ref[...]).astype(BF16)


def add_norm(x, s, r, gain, shift):
    rows = x.shape[0]
    return pl.pallas_call(
        add_norm_kernel,
        out_shape=(
            jax.ShapeDtypeStruct((rows, D), F32),
            jax.ShapeDtypeStruct((rows, D), BF16),
        ),
        in_specs=[whole((rows, D))] * 3 + [whole((1, D))] * 2,
        out_specs=(whole((rows, D)), whole((rows, D))),
        grid=(1,),
        compiler_params=params(16),
        cost_estimate=cost(10 * rows * D, 14 * rows * D),
        name="add_norm",
    )(x, s, r, gain, shift)


def norm_back_kernel(x0_ref, x1_ref, s_ref, r_ref, prev_ref, g_ref, d_ref, low_ref, sums_ref):
    x = jnp.concatenate([x0_ref[...], x1_ref[...]], axis=0).astype(F32)
    da = s_ref[...].astype(F32) + r_ref[...].astype(F32)
    centered, r = moments(x)
    xh = centered * r
    e = da * g_ref[...]
    mean_e = jnp.mean(e, axis=-1, keepdims=True)
    mean_ex = jnp.mean(e * xh, axis=-1, keepdims=True)
    out = prev_ref[...].astype(F32) + r * (e - mean_e - xh * mean_ex)
    d_ref[...] = out
    low_ref[...] = out.astype(BF16)
    sums_ref[0:1, :] = jnp.sum(da * xh, axis=0, keepdims=True)
    sums_ref[1:2, :] = jnp.sum(da, axis=0, keepdims=True)


def norm_back(x0, x1, s, r, prev, gain):
    rows = 2 * OWN
    return pl.pallas_call(
        norm_back_kernel,
        out_shape=(
            jax.ShapeDtypeStruct((rows, D), F32),
            jax.ShapeDtypeStruct((rows, D), BF16),
            jax.ShapeDtypeStruct((2, D), F32),
        ),
        in_specs=[whole((OWN, D))] * 2 + [whole((rows, D))] * 3 + [whole((1, D))],
        out_specs=(whole((rows, D)), whole((rows, D)), whole((2, D))),
        grid=(1,),
        compiler_params=params(32),
        cost_estimate=cost(20 * rows * D, 18 * rows * D),
        name="norm_back",
    )(x0, x1, s, r, prev, gain)


def rot(x, cos, sin):
    return x * cos + pltpu.roll(x, E // 2, 1) * sin


def allowed(core, q_start, rows, k_start, columns):
    flip = core * OWN
    q = (lax.broadcasted_iota(jnp.int32, (rows, columns), 0) + q_start) ^ flip
    k = (lax.broadcasted_iota(jnp.int32, (rows, columns), 1) + k_start) ^ flip
    return k <= q


def softmax(s):
    top = jnp.max(s, axis=-1, keepdims=True)
    e = jnp.exp(s - top)
    return e / jnp.sum(e, axis=-1, keepdims=True)


def attend_kernel(chunk, core_ref, am_ref, at_ref, w_ref, wo_ref, cos_ref, sin_ref, *rest):
    if chunk:
        before_ref, qkv_ref, o_ref, pm_ref, pt_ref, acc = rest
    else:
        qkv_ref, o_ref, pm_ref, pt_ref, acc = rest
    step = pl.program_id(0)
    a = jnp.concatenate([am_ref[...], at_ref[...]], axis=0)
    w = jnp.concatenate([w_ref[0, 0], w_ref[0, 1], w_ref[0, 2]], axis=1)
    p = dot(a, w)
    cos, sin = cos_ref[...], sin_ref[...]
    q = (rot(p[:, :E], cos, sin) * SCALE).astype(BF16)
    k = rot(p[:, E : 2 * E], cos, sin).astype(BF16)
    v = p[:, 2 * E :].astype(BF16)
    qkv_ref[0], qkv_ref[1], qkv_ref[2] = q, k, v
    if chunk:
        k = jnp.concatenate([before_ref[1], k], axis=0)
        v = jnp.concatenate([before_ref[2], v], axis=0)
    s = dot_t(q, k)
    s = jnp.where(allowed(core_ref[0], chunk * HALF, HALF, 0, s.shape[1]), s, MASKED)
    o = dot(softmax(s).astype(BF16), v).astype(BF16)
    o_ref[...] = o
    part = dot(o, wo_ref[0])

    @pl.when(step == 0)
    def _():
        acc[...] = part

    @pl.when(step == 1)
    def _():
        acc[...] += part

    @pl.when(step == HEADS - 1)
    def _():
        total = acc[...] + part
        pm_ref[...] = total[:OWN].astype(BF16)
        pt_ref[...] = total[OWN:].astype(BF16)


def attend(layer, chunk, core, am, at, w_qkv, w_out, cos, sin, before):
    head = pl.BlockSpec((3, HALF, E), lambda h: (0, 0, h))
    tables = pl.BlockSpec((HALF, E), lambda h: (chunk, 0))
    piece = whole((OWN, D))
    return pl.pallas_call(
        functools.partial(attend_kernel, chunk),
        out_shape=(
            jax.ShapeDtypeStruct((3, HALF, HID), BF16),
            jax.ShapeDtypeStruct((HALF, HID), BF16),
            jax.ShapeDtypeStruct((OWN, D), BF16),
            jax.ShapeDtypeStruct((OWN, D), BF16),
        ),
        in_specs=[
            SMEM,
            am[1],
            at[1],
            pl.BlockSpec((1, 3, D, E), lambda h: (layer, 0, 0, h)),
            pl.BlockSpec((1, E, D), lambda h: (layer, h, 0)),
            tables,
            tables,
        ]
        + ([head] if chunk else []),
        out_specs=(head, pl.BlockSpec((HALF, E), lambda h: (0, h)), piece, piece),
        scratch_shapes=[pltpu.VMEM((HALF, D), F32)],
        grid=(HEADS,),
        compiler_params=params(32),
        cost_estimate=cost(2 * HALF * D * 4 * HID, 2 * 4 * HID * D + 8 * HALF * D),
        name="attend",
    )(core, am[0], at[0], w_qkv, w_out, cos, sin, *([before] if chunk else []))


def attend_back_kernel(
    core_ref, gm_ref, gt_ref, w_ref, wo_ref, cos_ref, sin_ref, c0_ref, c1_ref, d_ref, pm_ref, pt_ref, acc
):
    step = pl.program_id(0)
    g0 = jnp.concatenate([gm_ref[:OWN], gt_ref[:OWN]], axis=0)
    g1 = jnp.concatenate([gm_ref[OWN:], gt_ref[OWN:]], axis=0)
    do0 = dot_t(g0, wo_ref[0]).astype(BF16)
    do1 = dot_t(g1, wo_ref[0]).astype(BF16)
    k = jnp.concatenate([c0_ref[1], c1_ref[1]], axis=0)
    v = jnp.concatenate([c0_ref[2], c1_ref[2]], axis=0)
    core = core_ref[0]

    def block(chunk, q, do, keys, values):
        s = dot_t(q, keys)
        s = jnp.where(allowed(core, chunk * HALF, HALF, 0, s.shape[1]), s, MASKED)
        prob = softmax(s)
        dp = dot_t(do, values)
        ds = (prob * (dp - jnp.sum(prob * dp, axis=-1, keepdims=True))).astype(BF16)
        return dot(ds, keys), t_dot(ds, q), t_dot(prob.astype(BF16), do)

    dq1, dk1, dv1 = block(1, c1_ref[0], do1, k, v)
    dq0, dk0, dv0 = block(0, c0_ref[0], do0, c0_ref[1], c0_ref[2])
    cos, sin = cos_ref[...], -sin_ref[...]
    dq = (rot(jnp.concatenate([dq0, dq1], axis=0), cos, sin) * SCALE).astype(BF16)
    dk = jnp.concatenate([dk0 + dk1[:HALF], dk1[HALF:]], axis=0)
    dk = rot(dk, cos, sin).astype(BF16)
    dv = jnp.concatenate([dv0 + dv1[:HALF], dv1[HALF:]], axis=0).astype(BF16)
    d_ref[0], d_ref[1], d_ref[2] = dq, dk, dv
    w = jnp.concatenate([w_ref[0, 0], w_ref[0, 1], w_ref[0, 2]], axis=1)
    part = dot_t(jnp.concatenate([dq, dk, dv], axis=1), w)

    @pl.when(step == 0)
    def _():
        acc[...] = part

    @pl.when(step == 1)
    def _():
        acc[...] += part

    @pl.when(step == HEADS - 1)
    def _():
        total = acc[...] + part
        split_rows(total, pm_ref, pt_ref)


def split_rows(total, pm_ref, pt_ref):
    pm_ref[:OWN] = total[:OWN].astype(BF16)
    pt_ref[:OWN] = total[OWN : 2 * OWN].astype(BF16)
    pm_ref[OWN:] = total[2 * OWN : 3 * OWN].astype(BF16)
    pt_ref[OWN:] = total[3 * OWN :].astype(BF16)


def attend_back(layer, core, gm, gt, w_qkv, w_out, cos, sin, saved0, saved1):
    rows = 2 * HALF
    head = pl.BlockSpec((3, HALF, E), lambda h: (0, 0, h))
    piece = whole((HALF, D))
    return pl.pallas_call(
        attend_back_kernel,
        out_shape=(
            jax.ShapeDtypeStruct((3, rows, HID), BF16),
            jax.ShapeDtypeStruct((HALF, D), BF16),
            jax.ShapeDtypeStruct((HALF, D), BF16),
        ),
        in_specs=[
            SMEM,
            piece,
            piece,
            pl.BlockSpec((1, 3, D, E), lambda h: (layer, 0, 0, h)),
            pl.BlockSpec((1, E, D), lambda h: (layer, h, 0)),
            whole((rows, E)),
            whole((rows, E)),
            head,
            head,
        ],
        out_specs=(pl.BlockSpec((3, rows, E), lambda h: (0, 0, h)), piece, piece),
        scratch_shapes=[pltpu.VMEM((rows, D), F32)],
        grid=(HEADS,),
        compiler_params=params(40),
        cost_estimate=cost(2 * rows * D * 5 * HID, 2 * 4 * HID * D + 8 * rows * D),
        name="attend_back",
    )(core, gm, gt, w_qkv, w_out, cos, sin, saved0, saved1)


def feed_kernel(width_ref, am_ref, at_ref, up_ref, down_ref, hid_ref, slope_ref, pm_ref, pt_ref, acc):
    step = pl.program_id(0)
    a = jnp.concatenate([am_ref[...], at_ref[...]], axis=0)
    u = dot(a, up_ref[0])
    place = lax.broadcasted_iota(jnp.int32, u.shape, 1) + step * FB
    keep = place < width_ref[0]
    square = u * u
    t = jnp.tanh(C1 * (u + C2 * u * square))
    hid = jnp.where(keep, 0.5 * u * (1.0 + t), 0.0).astype(BF16)
    slope = 0.5 * (1.0 + t) + 0.5 * u * (1.0 - t * t) * (C1 * (1.0 + 3.0 * C2 * square))
    slope_ref[...] = jnp.where(keep, slope, 0.0).astype(BF16)
    hid_ref[...] = hid
    part = dot(hid, down_ref[0])

    @pl.when(step == 0)
    def _():
        acc[...] = part

    @pl.when(step > 0)
    def _():
        acc[...] += part

    @pl.when(step == SLICE // FB - 1)
    def _():
        pm_ref[...] = acc[:OWN].astype(BF16)
        pt_ref[...] = acc[OWN:].astype(BF16)


def feed(layer, width, am, at, w_up, w_down):
    piece = whole((OWN, D))
    block = pl.BlockSpec((HALF, FB), lambda j: (0, j))
    return pl.pallas_call(
        feed_kernel,
        out_shape=(
            jax.ShapeDtypeStruct((HALF, SLICE), BF16),
            jax.ShapeDtypeStruct((HALF, SLICE), BF16),
            jax.ShapeDtypeStruct((OWN, D), BF16),
            jax.ShapeDtypeStruct((OWN, D), BF16),
        ),
        in_specs=[
            SMEM,
            piece,
            piece,
            pl.BlockSpec((1, D, FB), lambda j: (layer, 0, j)),
            pl.BlockSpec((1, FB, D), lambda j: (layer, j, 0)),
        ],
        out_specs=(block, block, piece, piece),
        scratch_shapes=[pltpu.VMEM((HALF, D), F32)],
        grid=(SLICE // FB,),
        compiler_params=params(32),
        cost_estimate=cost(4 * HALF * D * SLICE, 4 * SLICE * D + 8 * HALF * D),
        name="feed",
    )(width, am, at, w_up, w_down)


def feed_back_kernel(gm_ref, gt_ref, down_ref, up_ref, slope0_ref, slope1_ref, du_ref, pm_ref, pt_ref, acc):
    step = pl.program_id(0)
    g = jnp.concatenate([gm_ref[:OWN], gt_ref[:OWN], gm_ref[OWN:], gt_ref[OWN:]], axis=0)
    dhid = dot_t(g, down_ref[0])
    slope = jnp.concatenate([slope0_ref[...], slope1_ref[...]], axis=0).astype(F32)
    du = (dhid * slope).astype(BF16)
    du_ref[...] = du
    part = dot_t(du, up_ref[0])

    @pl.when(step == 0)
    def _():
        acc[...] = part

    @pl.when(step > 0)
    def _():
        acc[...] += part

    @pl.when(step == SLICE // FB - 1)
    def _():
        split_rows(acc[...], pm_ref, pt_ref)


def feed_back(layer, gm, gt, w_up, w_down, slope0, slope1):
    rows = 2 * HALF
    piece = whole((HALF, D))
    block = pl.BlockSpec((HALF, FB), lambda j: (0, j))
    return pl.pallas_call(
        feed_back_kernel,
        out_shape=(
            jax.ShapeDtypeStruct((rows, SLICE), BF16),
            jax.ShapeDtypeStruct((HALF, D), BF16),
            jax.ShapeDtypeStruct((HALF, D), BF16),
        ),
        in_specs=[
            piece,
            piece,
            pl.BlockSpec((1, FB, D), lambda j: (layer, j, 0)),
            pl.BlockSpec((1, D, FB), lambda j: (layer, 0, j)),
            block,
            block,
        ],
        out_specs=(pl.BlockSpec((rows, FB), lambda j: (0, j)), piece, piece),
        scratch_shapes=[pltpu.VMEM((rows, D), F32)],
        grid=(SLICE // FB,),
        compiler_params=params(40),
        cost_estimate=cost(4 * rows * D * SLICE, 4 * SLICE * D + 8 * rows * D),
        name="feed_back",
    )(gm, gt, w_down, w_up, slope0, slope1)


NB = 384


def rows_of(first, d, place_ref):
    at = lax.rem(place_ref[0 if first else 1] + d, 4)
    offsets = []
    for major in range(2):
        for minor in range(4):
            block = (major * 4 + minor) * 4 + at if first else (major * 4 + at) * 4 + minor
            offsets.append(pl.multiple_of(block * 48, 16))
    return offsets


def assemble(refs):
    if len(refs) == 2:
        m, t = refs
        return [m[:OWN], t[:OWN], m[OWN:], t[OWN:]]
    return [r[...] for r in refs]


def grad_kernel(first, counts, steps, place_ref, *refs):
    lefts, refs = refs[: sum(counts)], refs[sum(counts) :]
    count = len(steps)
    rights, refs = refs[: sum(n for n, _ in steps)], refs[sum(n for n, _ in steps) :]
    outs, (turned, total) = refs[:4], refs[4:]
    step = pl.program_id(0)
    start = 0
    at_left = at_right = 0
    for number in range(count):
        left = lefts[at_left : at_left + counts[number]]
        right = rights[at_right : at_right + steps[number][0]]
        at_left += counts[number]
        at_right += steps[number][0]

        @pl.when(step == start)
        def _():
            turned[...] = jnp.concatenate(assemble(left), axis=0).T

        @pl.when((step >= start) & (step < start + steps[number][1]))
        def _():
            b = jnp.concatenate([r[0] if len(r.shape) == 3 else r[...] for r in right], axis=0)
            total[...] = dot(turned[...], b).astype(BF16)

        start += steps[number][1]
    for d in range(4):
        for place, offset in enumerate(rows_of(first, d, place_ref)):
            outs[d][place * 48 : (place + 1) * 48, :] = total[pl.ds(offset, 48), :]


def grads(first, place, terms):
    lefts, specs, rights, right_specs = [], [], [], []
    counts, steps, start = [], [], 0
    for left, right, number in terms:
        lefts += left
        specs += [whole(a.shape) for a in left]
        counts.append(len(left))
        steps.append((len(right), number))
        for array, block, index in right:
            rights.append(array)
            right_specs.append(
                pl.BlockSpec(
                    block,
                    lambda j, s=start, n=number, index=index: index(jnp.clip(j - s, 0, n - 1)),
                )
            )
        start += number
    out = pl.BlockSpec((384, NB), lambda j: (0, j))
    columns = start * NB
    return pl.pallas_call(
        functools.partial(grad_kernel, first, counts, steps),
        out_shape=(jax.ShapeDtypeStruct((384, columns), BF16),) * 4,
        in_specs=[SMEM] + specs + right_specs,
        out_specs=(out,) * 4,
        scratch_shapes=[pltpu.VMEM((D, 2 * HALF), BF16), pltpu.VMEM((D, NB), BF16)],
        grid=(start,),
        compiler_params=params(40),
        cost_estimate=cost(2 * 2 * HALF * D * columns, 2 * D * columns + 2 * 2 * HALF * (columns + D)),
        name="grads",
    )(place, *lefts, *rights)


def sum_kernel(first, place_ref, a_ref, b_ref, c_ref, d_ref, o0, o1, o2, o3, total):
    t = a_ref[...].astype(F32) + b_ref[...].astype(F32) + c_ref[...].astype(F32) + d_ref[...].astype(F32)
    total[...] = t.astype(BF16)
    here = place_ref[1 if first else 0]
    for d, out in enumerate((o0, o1, o2, o3)):
        at = lax.rem(here + d, 4)
        for major in range(2):
            offset = pl.multiple_of((major * 4 + at) * 48, 16)
            out[major * 48 : (major + 1) * 48, :] = total[pl.ds(offset, 48), :]


def sum_ring(first, place, parts):
    columns = parts[0].shape[1]
    spec = pl.BlockSpec((384, NB), lambda j: (0, j))
    out = pl.BlockSpec((96, NB), lambda j: (0, j))
    return pl.pallas_call(
        functools.partial(sum_kernel, first),
        out_shape=(jax.ShapeDtypeStruct((96, columns), BF16),) * 4,
        in_specs=[SMEM] + [spec] * 4,
        out_specs=(out,) * 4,
        scratch_shapes=[pltpu.VMEM((384, NB), BF16)],
        grid=(columns // NB,),
        compiler_params=params(16),
        cost_estimate=cost(4 * 384 * columns, 10 * 384 * columns),
        name="sum_ring",
    )(place, *parts)


def last_kernel(place_ref, *refs):
    ins, (keep, away, total) = refs[:-3], refs[-3:]
    half = len(ins) // 2
    here = place_ref[2]
    columns = ins[0].shape[1]
    for number in range(2):
        t = sum(r[...].astype(F32) for r in ins[number * half : (number + 1) * half])
        total[:, number * columns : (number + 1) * columns] = t
    keep[...] = total[pl.ds(pl.multiple_of(here * 48, 16), 48), :]
    away[...] = total[pl.ds(pl.multiple_of((1 - here) * 48, 16), 48), :].astype(BF16)


def sum_last(place, parts_x, parts_y):
    columns = parts_x[0].shape[1]
    return pl.pallas_call(
        last_kernel,
        out_shape=(
            jax.ShapeDtypeStruct((48, 2 * columns), F32),
            jax.ShapeDtypeStruct((48, 2 * columns), BF16),
        ),
        in_specs=[SMEM] + [whole((96, columns))] * 8,
        out_specs=(whole((48, 2 * columns)),) * 2,
        scratch_shapes=[pltpu.VMEM((96, 2 * columns), F32)],
        grid=(1,),
        compiler_params=params(24),
        cost_estimate=cost(8 * 96 * columns, 24 * 96 * columns),
        name="sum_last",
    )(place, *parts_x, *parts_y)


def reduce_pair(place, parts_x, parts_y):
    got_x = [parts_x[0]] + [send(parts_x[d], x_by(d)) for d in (1, 2, 3)]
    got_y = [parts_y[0]] + [send(parts_y[d], y_by(d)) for d in (1, 2, 3)]
    next_x = sum_ring(True, place, got_x)
    next_y = sum_ring(False, place, got_y)
    got_x = [next_x[0]] + [send(next_x[d], y_by(d)) for d in (1, 2, 3)]
    got_y = [next_y[0]] + [send(next_y[d], x_by(d)) for d in (1, 2, 3)]
    keep, away = sum_last(place, got_x, got_y)
    return keep + send(away, ZLO).astype(F32)


def body(tokens, norm_gain, norm_shift, w_qkv, w_out, w_up, w_down, granularity, cotangent):
    zl, y, x, zh, c = (lax.axis_index(a) for a in AXES)
    layers = w_qkv.shape[0]
    core = c.reshape(1).astype(jnp.int32)
    place = jnp.stack([x, y, zl]).astype(jnp.int32)
    width = FF // 8 * 2 ** granularity[0, 0] - (zh * 2 + c) * SLICE
    width = width.reshape(1).astype(jnp.int32)
    w_qkv = jnp.transpose(w_qkv, (0, 2, 1, 3))
    low_chip = zh == 0

    positions = (jnp.arange(2 * HALF, dtype=jnp.int32) ^ (c * OWN)).astype(F32)[:, None]
    half = E // 2
    frequency = BASE ** (-jnp.arange(half, dtype=F32) / half)
    angles = positions * frequency[None, :]
    cos = jnp.cos(angles)
    sin = jnp.sin(angles)
    cos = jnp.concatenate([cos, cos], axis=1)
    sin = jnp.concatenate([-sin, sin], axis=1)

    def gain(layer, member):
        return norm_gain[layer, member][None, :]

    def shift(layer, member):
        return norm_shift[layer, member][None, :]

    def both_chunks(own):
        other = send(own, FAR)
        return jnp.where(low_chip, own, other), jnp.where(low_chip, other, own)

    def exchange(mine, theirs):
        s = mine.astype(F32) + send(theirs, CORE).astype(F32)
        s = s.astype(BF16)
        return s, send(s, FAR)

    whole_piece = whole((OWN, D))

    def swap(a):
        return (a, whole_piece), (send(a, CORE), whole_piece)

    stream = list(both_chunks(tokens))
    normed = [swap(norm(stream[k], gain(0, 0), shift(0, 0))) for k in range(2)]
    saved = []
    last = None
    for layer in range(layers):
        keep = {"stream": list(stream), "normed": normed}
        qkv, mixture, sums = [None] * 2, [None] * 2, [None] * 2
        mid, normed_two = [None] * 2, [None] * 2
        hid, slope = [None] * 2, [None] * 2
        for k in range(2):
            qkv[k], mixture[k], pm, pt = attend(
                layer, k, core, *normed[k], w_qkv, w_out, cos, sin, qkv[0]
            )
            sums[k] = exchange(pm, pt)
        for k in range(2):
            mid[k], a = add_norm(stream[k], *sums[k], gain(layer, 1), shift(layer, 1))
            normed_two[k] = swap(a)
        following = [None] * 2
        parts = [None] * 2
        for k in range(2):
            am, at = normed_two[k]
            hid[k], slope[k], pm, pt = feed(layer, width, am[0], at[0], w_up, w_down)
            if layer < layers - 1:
                sums[k] = exchange(pm, pt)
            else:
                parts[k] = (pm, pt)
        keep.update(qkv=qkv, mixture=mixture, mid=mid, normed_two=normed_two, hid=hid, slope=slope)
        saved.append(keep)
        if layer < layers - 1:
            for k in range(2):
                stream[k], a = add_norm(mid[k], *sums[k], gain(layer + 1, 0), shift(layer + 1, 0))
                following[k] = swap(a)
            normed = following
        else:
            s = [
                parts[k][0].astype(F32) + send(parts[k][1], CORE).astype(F32) for k in range(2)
            ]
            ours = jnp.where(low_chip, s[0], s[1])
            away = jnp.where(low_chip, s[1], s[0]).astype(BF16)
            base = jnp.where(low_chip, mid[0], mid[1])
            last = (base + (ours + send(away, FAR).astype(F32))).astype(BF16)

    gradient = jnp.concatenate(both_chunks(cotangent), axis=0)
    gm = gradient
    gt = send(gm, CORE)
    weight_grads = [None] * layers
    norm_sums = [[None, None] for _ in range(layers)]
    for layer in reversed(range(layers)):
        kept = saved[layer]
        a_two = [p[0] for k in range(2) for p in kept["normed_two"][k]]
        a_one = [p[0] for k in range(2) for p in kept["normed"][k]]
        du, pm, pt = feed_back(layer, gm, gt, w_up, w_down, *kept["slope"])
        s, r = exchange(pm, pt)

        def column(j):
            return (0, j)

        up_parts = grads(True, place, [(a_two, [(du, (2 * HALF, NB), column)], SLICE // NB)])
        down_parts = grads(
            False, place, [([gm, gt], [(h, (HALF, NB), column) for h in kept["hid"]], SLICE // NB)]
        )
        feed_grad = reduce_pair(place, up_parts, down_parts)
        gradient, gm, norm_sums[layer][1] = norm_back(*kept["mid"], s, r, gradient, gain(layer, 1))
        gt = send(gm, CORE)
        dqkv, pm, pt = attend_back(layer, core, gm, gt, w_qkv, w_out, cos, sin, *kept["qkv"])
        s, r = exchange(pm, pt)
        first = grads(
            True, place, [(a_one, [(dqkv, (1, 2 * HALF, NB), lambda j: (j, 0, 0))], 2)]
        )
        second = grads(
            False,
            place,
            [
                (a_one, [(dqkv, (1, 2 * HALF, NB), lambda j: (2, 0, 0))], 1),
                ([gm, gt], [(m, (HALF, NB), lambda j: (0, 0)) for m in kept["mixture"]], 1),
            ],
        )
        attend_grad = reduce_pair(place, first, second)
        gradient, gm, norm_sums[layer][0] = norm_back(
            *kept["stream"], s, r, gradient, gain(layer, 0)
        )
        if layer:
            gt = send(gm, CORE)
        weight_grads[layer] = (feed_grad, attend_grad)

    input_grad = jnp.where(low_chip, gradient[:OWN], gradient[OWN:])
    sums = jnp.stack([norm_sums[layer][member] for layer in range(layers) for member in range(2)])
    for perm in (CORE, x_flip(1), x_flip(2), y_flip(1), y_flip(2), ZLO):
        sums = sums + send(sums, perm)
    sums = sums.reshape(layers, 2, 2, D)
    gain_grads, shift_grads = sums[:, :, 0], sums[:, :, 1]

    feed_grads = jnp.stack([w[0] for w in weight_grads])
    attend_grads = jnp.stack([w[1] for w in weight_grads])
    grad_up = feed_grads[:, :, :SLICE]
    grad_down = jnp.swapaxes(feed_grads[:, :, SLICE:], 1, 2)
    grad_qkv = attend_grads[:, :, : 3 * HID].reshape(layers, 48, 3, HID)
    grad_out = jnp.swapaxes(attend_grads[:, :, 3 * HID :], 1, 2)
    return (
        last,
        input_grad,
        grad_qkv,
        grad_out,
        grad_up,
        grad_down,
        gain_grads,
        shift_grads,
        shift_grads[:, 1, :],
    )


def solution(mesh):
    fine = Mesh(mesh.devices.reshape(SIZES), AXES)
    rows = P(AXES, None)
    dp, tensor = AXES[:3], AXES[3:]
    return jax.shard_map(
        body,
        mesh=fine,
        in_specs=(
            rows,
            P(),
            P(),
            P(None, None, None, tensor),
            P(None, tensor, None),
            P(None, None, tensor),
            P(None, tensor, None),
            P(dp, None),
            rows,
        ),
        out_specs=(
            rows,
            rows,
            P(None, dp, None, tensor),
            P(None, tensor, dp),
            P(None, dp, tensor),
            P(None, tensor, dp),
            P(),
            P(),
            P(),
        ),
        check_vma=False,
    )
```

time: 1410 us -> 621 us (0.44)
  waiting for transfers between devices: 1000 us -> 192 us
  starting transfers between devices: 2.53 us -> 182 us
  Pallas kernels: 0 us -> 171 us
  matrix products: 130 us -> 0 us
  other arithmetic: 87.6 us -> 11.4 us
  blocking collectives: 68.2 us -> 0 us
  local copies, waits for them, and re-layouts: 78.1 us -> 51 us
    reduce_scatter x10 -> x0, waiting for transfers between devices: 582 us -> none  [the longest x1 175 us: body(): lax.psum_scatter(stacked[2].astype(jnp.bfloat16), 'dp', scatter_dimension...]
    unnamed x20 -> x0, waiting for transfers between devices: 247 us -> none
    ppermute x0 -> x95, waiting for transfers between devices: none -> 192 us  [send(): return lax.ppermute(values, AXES, perm)]
    ppermute x0 -> x95, starting transfers between devices: none -> 182 us  [send(): return lax.ppermute(values, AXES, perm)]
    all_gather x8 -> x0, waiting for transfers between devices: 176 us -> none  [the longest x4 92.1 us: gather_rows(): return lax.all_gather(values, 'tensor', axis=0, tiled=True)]
    pallas_call x0 -> x44, Pallas kernels: none -> 171 us  [the longest x8 44.9 us: grads(): pl.pallas_call(functools.partial(grad_kernel, first, counts, steps), out_...]
    dot_general x36 -> x0, matrix products: 130 us -> none  [the longest x2 15.9 us: layer_back(): jnp.einsum('td,fd->tf', feed_gradient, down_weight, preferred_element_typ...]
    psum x1 -> x0, blocking collectives: 68.2 us -> none  [body(): lax.psum((gain_grads, shift_grads), ('dp', 'tensor'))]
  transfers between devices with their start and end apart: 19 -> 95, of which waited for: 18 -> 37; matrix products, arithmetic and copies ran while one was open for 8% -> 2% of each run, Pallas kernels for 0% -> 24%
where the time goes in v1:
time: 621 us; the launch traced here: 611 us
  waiting for transfers between devices  192 us (31%)
  starting transfers between devices  182 us (29%)
  Pallas kernels  171 us (28%)
  local copies, waits for them, and re-layouts  51 us (8%)
  other arithmetic  11.4 us (2%)
    ppermute x95, waiting for transfers between devices, send(): return lax.ppermute(values, AXES, perm)  192 us
    ppermute x95, starting transfers between devices, send(): return lax.ppermute(values, AXES, perm)  182 us
    unnamed x283, local copies, waits for them, and re-layouts  48.5 us
    pallas_call x8, Pallas kernels, grads(): pl.pallas_call(functools.partial(grad_kernel, first, counts, steps), out_...  44.9 us
    pallas_call x4, Pallas kernels, feed(): pl.pallas_call(feed_kernel, out_shape=(jax.ShapeDtypeStruct((HALF, SLICE)...  28.8 us
    pallas_call x4, Pallas kernels, attend(): pl.pallas_call(functools.partial(attend_kernel, chunk), out_shape=(jax.Sh...  22.4 us
    pallas_call x2, Pallas kernels, feed_back(): pl.pallas_call(feed_back_kernel, out_shape=(jax.ShapeDtypeStruct((rows, S...  21.9 us
    pallas_call x2, Pallas kernels, attend_back(): pl.pallas_call(attend_back_kernel, out_shape=(jax.ShapeDtypeStruct((3, ro...  21.8 us
  transfers between devices with their start and end apart: 95, of which 37 were waited for; matrix products, arithmetic and copies ran while one was open for 2% of the time, Pallas kernels for 24%

profile of v1, /device:TPU:10, one launch (start us, length us, event | category | flops | bytes accessed | tf_op | source)
XLA Modules:
  0.0 611.1 jit_solution(13977685219178176633)
XLA Ops:
  6.2 7.7 %collective-permute-done = bf16[128,1536]{1,0:T(8,128)(2,1)S(1)} collective-permute-done((bf16[128,1536]{1,0:T(8,128)(2,1)}, bf16[128,1536]{1,0:T(8,128)(2,1)S(1)}, u32[]{:S(2)}, u32[]{:S(2)}) %collective-permute-start) | collective-permute-done | bytes 393248 | tf_op jit(solution)/shard_map/ppermute | solution.py:69
  37.5 8.9 %collective-permute-done.3.r_ref = bf16[128,1536]{1,0:T(8,128)(2,1)S(1)} collective-permute-done((bf16[128,1536]{1,0:T(8,128)(2,1)S(1)}, bf16[128,1536]{1,0:T(8,128)(2,1)S(1)}, u32[]{:S(2)}, u32[]{:S(2)}) %collective-permute-start.3) | collective-permute-done | bytes 393248 | tf_op jit(solution)/shard_map/ppermute | solution.py:69
  64.4 8.3 %feed.4 = (bf16[256,1536]{1,0:T(8,128)(2,1)S(1)}, bf16[256,1536]{1,0:T(8,128)(2,1)S(1)}, bf16[128,1536]{1,0:T(8,128)(2,1)S(1)}, bf16[128,1536]{1,0:T(8,128)(2,1)}) custom-call(s32[1]{0:T(128)} %bitcast.12.width_ref, bf16[128,1536]{1,0:T(8,128)(2,1)} %get-tuple-element.151.am_ref.refs_0_, bf16[128,1536]{1,0:T(8,128)(2,1)} %collective-permute-done.4.at_ref.refs_1_, ...), custom_call_target="tpu_custom_call" | custom-call | flops 2415919104 | bytes 12582912 | tf_op jit(solution)/shard_map/feed/pallas_call | solution.py:383
  79.7 7.5 %feed.5 = (bf16[256,1536]{1,0:T(8,128)(2,1)S(1)}, bf16[256,1536]{1,0:T(8,128)(2,1)S(1)}, bf16[128,1536]{1,0:T(8,128)(2,1)S(1)}, bf16[128,1536]{1,0:T(8,128)(2,1)S(1)}) custom-call(s32[1]{0:T(128)} %bitcast.12.width_ref, bf16[128,1536]{1,0:T(8,128)(2,1)} %get-tuple-element.163.am_ref.refs_2_, bf16[128,1536]{1,0:T(8,128)(2,1)} %collective-permute-done.13.at_ref.refs_3_, ...), custom_call_target="tpu_custom_call" | custom-call | flops 2415919104 | bytes 12582912 | tf_op jit(solution)/shard_map/feed/pallas_call | solution.py:383
  92.5 8.8 %collective-permute-done.6.r_ref = bf16[128,1536]{1,0:T(8,128)(2,1)S(1)} collective-permute-done((bf16[128,1536]{1,0:T(8,128)(2,1)S(1)}, bf16[128,1536]{1,0:T(8,128)(2,1)S(1)}, u32[]{:S(2)}, u32[]{:S(2)}) %collective-permute-start.6) | collective-permute-done | bytes 393248 | tf_op jit(solution)/shard_map/ppermute | solution.py:69
  130.7 8.6 %collective-permute-done.9.r_ref = bf16[128,1536]{1,0:T(8,128)(2,1)S(1)} collective-permute-done((bf16[128,1536]{1,0:T(8,128)(2,1)S(1)}, bf16[128,1536]{1,0:T(8,128)(2,1)S(1)}, u32[]{:S(2)}, u32[]{:S(2)}) %collective-permute-start.9) | collective-permute-done | bytes 393248 | tf_op jit(solution)/shard_map/ppermute | solution.py:69
  166.2 11.3 %feed_back.2 = (bf16[512,1536]{1,0:T(8,128)(2,1)S(1)}, bf16[256,1536]{1,0:T(8,128)(2,1)S(1)}, bf16[256,1536]{1,0:T(8,128)(2,1)S(1)}) custom-call(bf16[256,1536]{1,0:T(8,128)(2,1)S(1)} %pad_maximum_fusion.gm_ref.prev_ref.refs_0_, bf16[256,1536]{1,0:T(8,128)(2,1)S(1)} %collective-permute-done.25.gt_ref.refs_1_, bf16[2,1536,1536]{2,1,0:T(8,128)(2,1)} %down_ref.11, ...), custom_call_target="tpu_custom_call" | custom-call | flops 4831838208 | bytes 15728640 | tf_op jit(solution)/shard_map/feed_back/pallas_call | solution.py:433
  183.5 18.1 %collective-permute-done.27.r_ref = bf16[256,1536]{1,0:T(8,128)(2,1)S(1)} collective-permute-done((bf16[256,1536]{1,0:T(8,128)(2,1)S(1)}, bf16[256,1536]{1,0:T(8,128)(2,1)S(1)}, u32[]{:S(2)}, u32[]{:S(2)}) %collective-permute-start.27) | collective-permute-done | bytes 786464 | tf_op jit(solution)/shard_map/ppermute | solution.py:69
  206.4 11.0 %attend_back.2 = (bf16[3,512,384]{2,1,0:T(8,128)(2,1)S(1)}, bf16[256,1536]{1,0:T(8,128)(2,1)S(1)}, bf16[256,1536]{1,0:T(8,128)(2,1)S(1)}) custom-call(s32[1]{0:T(128)} %bitcast.core_ref, bf16[256,1536]{1,0:T(8,128)(2,1)S(1)} %get-tuple-element.182.gm_ref.refs_4_, bf16[256,1536]{1,0:T(8,128)(2,1)S(1)} %collective-permute-done.28.gt_ref.refs_5_, ...), custom_call_target="tpu_custom_call" | custom-call | flops 3019898880 | bytes 11010048 | tf_op jit(solution)/shard_map/attend_back/pallas_call | solution.py:325
  229.8 6.8 %grads.14 = (bf16[384,1536]{1,0:T(8,128)(2,1)S(1)}, bf16[384,1536]{1,0:T(8,128)(2,1)S(1)}, bf16[384,1536]{1,0:T(8,128)(2,1)}, bf16[384,1536]{1,0:T(8,128)(2,1)}) custom-call(s32[3]{0:T(128)S(1)} %pad_add_fusion.place_ref, bf16[128,1536]{1,0:T(8,128)(2,1)S(1)} %copy-done.75, bf16[128,1536]{1,0:T(8,128)(2,1)S(1)} %copy-done.77, ...), custom_call_target="tpu_custom_call" | custom-call | flops 2415919104 | bytes 7864320 | tf_op jit(solution)/shard_map/grads/pallas_call | solution.py:525
  250.9 6.8 %grads.15 = (bf16[384,1536]{1,0:T(8,128)(2,1)S(1)}, bf16[384,1536]{1,0:T(8,128)(2,1)S(1)}, bf16[384,1536]{1,0:T(8,128)(2,1)}, bf16[384,1536]{1,0:T(8,128)(2,1)}) custom-call(s32[3]{0:T(128)S(1)} %pad_add_fusion.place_ref, bf16[256,1536]{1,0:T(8,128)(2,1)S(1)} %copy-done.11, bf16[256,1536]{1,0:T(8,128)(2,1)S(1)} %copy-done.67, ...), custom_call_target="tpu_custom_call" | custom-call | flops 2415919104 | bytes 7864320 | tf_op jit(solution)/shard_map/grads/pallas_call | solution.py:525
  273.5 10.6 %feed_back.3 = (bf16[512,1536]{1,0:T(8,128)(2,1)S(1)}, bf16[256,1536]{1,0:T(8,128)(2,1)S(1)}, bf16[256,1536]{1,0:T(8,128)(2,1)S(1)}) custom-call(bf16[256,1536]{1,0:T(8,128)(2,1)S(1)} %get-tuple-element.187.gm_ref.refs_0_, bf16[256,1536]{1,0:T(8,128)(2,1)S(1)} %copy-done.60, bf16[2,1536,1536]{2,1,0:T(8,128)(2,1)} %down_ref.11, ...), custom_call_target="tpu_custom_call" | custom-call | flops 4831838208 | bytes 15728640 | tf_op jit(solution)/shard_map/feed_back/pallas_call | solution.py:433
  285.3 15.6 %collective-permute-done.78.d_ref = bf16[384,1536]{1,0:T(8,128)(2,1)S(1)} collective-permute-done((bf16[384,1536]{1,0:T(8,128)(2,1)}, bf16[384,1536]{1,0:T(8,128)(2,1)S(1)}, u32[]{:S(2)}, u32[]{:S(2)}) %collective-permute-start.78) | collective-permute-done | bytes 1179680 | tf_op jit(solution)/shard_map/ppermute | solution.py:69
  312.1 9.3 %collective-permute-done.84.d_ref = bf16[384,1536]{1,0:T(8,128)(2,1)S(1)} collective-permute-done((bf16[384,1536]{1,0:T(8,128)(2,1)}, bf16[384,1536]{1,0:T(8,128)(2,1)S(1)}, u32[]{:S(2)}, u32[]{:S(2)}) %collective-permute-start.84) | collective-permute-done | bytes 1179680 | tf_op jit(solution)/shard_map/ppermute | solution.py:69
  346.0 12.0 %collective-permute-done.86.refs_6_ = bf16[96,1536]{1,0:T(8,128)(2,1)S(1)} collective-permute-done((bf16[96,1536]{1,0:T(8,128)(2,1)S(1)}, bf16[96,1536]{1,0:T(8,128)(2,1)S(1)}, u32[]{:S(2)}, u32[]{:S(2)}) %collective-permute-start.86) | collective-permute-done | bytes 294944 | tf_op jit(solution)/shard_map/ppermute | solution.py:69
  358.7 13.6 %collective-permute-start.52 = (bf16[384,768]{1,0:T(8,128)(2,1)}, bf16[384,768]{1,0:T(8,128)(2,1)}, u32[]{:S(2)}, u32[]{:S(2)}) collective-permute-start(bf16[384,768]{1,0:T(8,128)(2,1)} %get-tuple-element.224), channel_id=1, source_target_pairs={{0,12},{1,13},{2,14},{3,15},{4,0},{5,1},{6,2},{7,3},{8,4},{9,5},{1... | collective-permute-start | bytes 1769480 | tf_op jit(solution)/shard_map/ppermute | solution.py:69
  379.7 7.8 %grads.12 = (bf16[384,1536]{1,0:T(8,128)(2,1)S(1)}, bf16[384,1536]{1,0:T(8,128)(2,1)}, bf16[384,1536]{1,0:T(8,128)(2,1)}, bf16[384,1536]{1,0:T(8,128)(2,1)}) custom-call(s32[3]{0:T(128)S(1)} %pad_add_fusion.place_ref, bf16[128,1536]{1,0:T(8,128)(2,1)} %get-tuple-element.151.am_ref.refs_0_, bf16[128,1536]{1,0:T(8,128)(2,1)} %collective-permute-done.4.at_ref.refs_1_, ...), custom_call_target="tpu_custom_call" | custom-call | flops 2415919104 | bytes 7864320 | tf_op jit(solution)/shard_map/grads/pallas_call | solution.py:525
  392.9 9.7 %collective-permute-start.53 = (bf16[96,768]{1,0:T(8,128)(2,1)S(1)}, bf16[96,768]{1,0:T(8,128)(2,1)S(1)}, u32[]{:S(2)}, u32[]{:S(2)}) collective-permute-start(bf16[96,768]{1,0:T(8,128)(2,1)S(1)} %get-tuple-element.226), channel_id=1, source_target_pairs={{0,16},{1,17},{2,18},{3,19},{4,20},{5,21},{6,22},{7,23},{8,24},{9,... | collective-permute-start | bytes 442376 | tf_op jit(solution)/shard_map/ppermute | solution.py:69
  420.1 23.4 %collective-permute-done.59.refs_5_ = bf16[96,768]{1,0:T(8,128)(2,1)S(1)} collective-permute-done((bf16[96,768]{1,0:T(8,128)(2,1)S(1)}, bf16[96,768]{1,0:T(8,128)(2,1)S(1)}, u32[]{:S(2)}, u32[]{:S(2)}) %collective-permute-start.59) | collective-permute-done | bytes 147488 | tf_op jit(solution)/shard_map/ppermute | solution.py:69
  447.9 6.9 %grads.13 = (bf16[384,1536]{1,0:T(8,128)(2,1)S(1)}, bf16[384,1536]{1,0:T(8,128)(2,1)}, bf16[384,1536]{1,0:T(8,128)(2,1)}, bf16[384,1536]{1,0:T(8,128)(2,1)}) custom-call(s32[3]{0:T(128)S(1)} %pad_add_fusion.place_ref, bf16[256,1536]{1,0:T(8,128)(2,1)S(1)} %copy-done.58, bf16[256,1536]{1,0:T(8,128)(2,1)S(1)} %copy-done.61, bf16[256,1536]{1,0:T(8,128)(2,1)S(1)} %copy-done.117, ...), custom_call_target="tpu_custom_call" | custom-call | flops 2415919104 | bytes 7864320 | tf_op jit(solution)/shard_map/grads/pallas_call | solution.py:525
  458.4 10.9 %attend_back.3 = (bf16[3,512,384]{2,1,0:T(8,128)(2,1)S(1)}, bf16[256,1536]{1,0:T(8,128)(2,1)S(1)}, bf16[256,1536]{1,0:T(8,128)(2,1)S(1)}) custom-call(s32[1]{0:T(128)} %bitcast.core_ref, bf16[256,1536]{1,0:T(8,128)(2,1)S(1)} %get-tuple-element.193.gm_ref.refs_4_, bf16[256,1536]{1,0:T(8,128)(2,1)S(1)} %collective-permute-done.34.gt_ref.refs_5_, ...), custom_call_target="tpu_custom_call" | custom-call | flops 3019898880 | bytes 11010048 | tf_op jit(solution)/shard_map/attend_back/pallas_call | solution.py:325
  476.3 8.3 %collective-permute-done.69.b_ref = bf16[384,1536]{1,0:T(8,128)(2,1)S(1)} collective-permute-done((bf16[384,1536]{1,0:T(8,128)(2,1)}, bf16[384,1536]{1,0:T(8,128)(2,1)S(1)}, u32[]{:S(2)}, u32[]{:S(2)}) %collective-permute-start.69) | collective-permute-done | bytes 1179680 | tf_op jit(solution)/shard_map/ppermute | solution.py:69
  486.1 22.1 %collective-permute-start.66 = (bf16[96,1536]{1,0:T(8,128)(2,1)S(1)}, bf16[96,1536]{1,0:T(8,128)(2,1)S(1)}, u32[]{:S(2)}, u32[]{:S(2)}) collective-permute-start(bf16[96,1536]{1,0:T(8,128)(2,1)S(1)} %get-tuple-element.247), channel_id=1, source_target_pairs={{0,16},{1,17},{2,18},{3,19},{4,20},{5,21},{6,22},{7,23},{8,24},{9,... | collective-permute-start | bytes 884744 | tf_op jit(solution)/shard_map/ppermute | solution.py:69
  566.3 8.3 %collective-permute-start.42 = (bf16[96,768]{1,0:T(8,128)(2,1)S(1)}, bf16[96,768]{1,0:T(8,128)(2,1)S(1)}, u32[]{:S(2)}, u32[]{:S(2)}) collective-permute-start(bf16[96,768]{1,0:T(8,128)(2,1)S(1)} %get-tuple-element.207), channel_id=1, source_target_pairs={{0,48},{1,49},{2,50},{3,51},{4,52},{5,53},{6,54},{7,55},{8,56},{9,... | collective-permute-start | bytes 442376 | tf_op jit(solution)/shard_map/ppermute | solution.py:69
  (534 shorter events, 345.5 us)
Async XLA Ops:
  236.6 28.9 %collective-permute-start.76 = (bf16[384,1536]{1,0:T(8,128)(2,1)S(1)}, bf16[384,1536]{1,0:T(8,128)(2,1)S(1)}, u32[]{:S(2)}, u32[]{:S(2)}) collective-permute-start(bf16[384,1536]{1,0:T(8,128)(2,1)S(1)} %get-tuple-element.264), channel_id=1, source_target_pairs={{0,4},{1,5},{2,6},{3,7},{4,8},{5,9},{6,10},{7,11},{8,12},{9,13},{1... | collective-permute-start | bytes 3538952 | tf_op jit(solution)/shard_map/ppermute | solution.py:69
  245.5 38.5 %collective-permute-start.77 = (bf16[384,1536]{1,0:T(8,128)(2,1)}, bf16[384,1536]{1,0:T(8,128)(2,1)S(1)}, u32[]{:S(2)}, u32[]{:S(2)}) collective-permute-start(bf16[384,1536]{1,0:T(8,128)(2,1)} %get-tuple-element.265), channel_id=1, source_target_pairs={{0,8},{1,9},{2,10},{3,11},{4,12},{5,13},{6,14},{7,15},{8,0},{9,1},... | collective-permute-start | bytes 3538952 | tf_op jit(solution)/shard_map/ppermute | solution.py:69
  249.4 51.5 %collective-permute-start.78 = (bf16[384,1536]{1,0:T(8,128)(2,1)}, bf16[384,1536]{1,0:T(8,128)(2,1)S(1)}, u32[]{:S(2)}, u32[]{:S(2)}) collective-permute-start(bf16[384,1536]{1,0:T(8,128)(2,1)} %get-tuple-element.266), channel_id=1, source_target_pairs={{0,12},{1,13},{2,14},{3,15},{4,0},{5,1},{6,2},{7,3},{8,4},{9,5},{1... | collective-permute-start | bytes 3538952 | tf_op jit(solution)/shard_map/ppermute | solution.py:69
  258.5 48.0 %collective-permute-start.82 = (bf16[384,1536]{1,0:T(8,128)(2,1)S(1)}, bf16[384,1536]{1,0:T(8,128)(2,1)S(1)}, u32[]{:S(2)}, u32[]{:S(2)}) collective-permute-start(bf16[384,1536]{1,0:T(8,128)(2,1)S(1)} %get-tuple-element.274), channel_id=1, source_target_pairs={{0,16},{1,17},{2,18},{3,19},{4,20},{5,21},{6,22},{7,23},{8,24},{9,... | collective-permute-start | bytes 3538952 | tf_op jit(solution)/shard_map/ppermute | solution.py:69
  265.5 46.6 %collective-permute-start.83 = (bf16[384,1536]{1,0:T(8,128)(2,1)}, bf16[384,1536]{1,0:T(8,128)(2,1)S(1)}, u32[]{:S(2)}, u32[]{:S(2)}) collective-permute-start(bf16[384,1536]{1,0:T(8,128)(2,1)} %get-tuple-element.275), channel_id=1, source_target_pairs={{0,32},{1,33},{2,34},{3,35},{4,36},{5,37},{6,38},{7,39},{8,40},{9,... | collective-permute-start | bytes 3538952 | tf_op jit(solution)/shard_map/ppermute | solution.py:69
  268.7 52.6 %collective-permute-start.84 = (bf16[384,1536]{1,0:T(8,128)(2,1)}, bf16[384,1536]{1,0:T(8,128)(2,1)S(1)}, u32[]{:S(2)}, u32[]{:S(2)}) collective-permute-start(bf16[384,1536]{1,0:T(8,128)(2,1)} %get-tuple-element.276), channel_id=1, source_target_pairs={{0,48},{1,49},{2,50},{3,51},{4,52},{5,53},{6,54},{7,55},{8,56},{9,... | collective-permute-start | bytes 3538952 | tf_op jit(solution)/shard_map/ppermute | solution.py:69
  284.1 46.7 %collective-permute-start.32 = (bf16[256,1536]{1,0:T(8,128)(2,1)S(1)}, bf16[256,1536]{1,0:T(8,128)(2,1)}, u32[]{:S(2)}, u32[]{:S(2)}) collective-permute-start(bf16[256,1536]{1,0:T(8,128)(2,1)S(1)} %get-tuple-element.191), channel_id=1, source_target_pairs={{0,1},{1,0},{2,3},{3,2},{4,5},{5,4},{6,7},{7,6},{8,9},{9,8},{10,11... | collective-permute-start | bytes 2359304 | tf_op jit(solution)/shard_map/ppermute | solution.py:69
  330.8 43.9 %collective-permute-start.50 = (bf16[384,768]{1,0:T(8,128)(2,1)S(1)}, bf16[384,768]{1,0:T(8,128)(2,1)S(1)}, u32[]{:S(2)}, u32[]{:S(2)}) collective-permute-start(bf16[384,768]{1,0:T(8,128)(2,1)S(1)} %get-tuple-element.222), channel_id=1, source_target_pairs={{0,4},{1,5},{2,6},{3,7},{4,8},{5,9},{6,10},{7,11},{8,12},{9,13},{1... | collective-permute-start | bytes 1769480 | tf_op jit(solution)/shard_map/ppermute | solution.py:69
  333.5 54.0 %collective-permute-start.33 = (bf16[256,1536]{1,0:T(8,128)(2,1)S(1)}, bf16[256,1536]{1,0:T(8,128)(2,1)S(1)}, u32[]{:S(2)}, u32[]{:S(2)}) collective-permute-start(bf16[256,1536]{1,0:T(8,128)(2,1)S(1)} %add_convert_fusion.1.s_ref), channel_id=1, source_target_pairs={{0,2},{1,3},{2,0},{3,1},{4,6},{5,7},{6,4},{7,5},{8,10},{9,11},{10,... | collective-permute-start | bytes 2359304 | tf_op jit(solution)/shard_map/ppermute | solution.py:69
  333.9 53.6 %collective-permute-start.51 = (bf16[384,768]{1,0:T(8,128)(2,1)S(1)}, bf16[384,768]{1,0:T(8,128)(2,1)S(1)}, u32[]{:S(2)}, u32[]{:S(2)}) collective-permute-start(bf16[384,768]{1,0:T(8,128)(2,1)S(1)} %get-tuple-element.223), channel_id=1, source_target_pairs={{0,8},{1,9},{2,10},{3,11},{4,12},{5,13},{6,14},{7,15},{8,0},{9,1},... | collective-permute-start | bytes 1769480 | tf_op jit(solution)/shard_map/ppermute | solution.py:69
  339.2 33.1 %collective-permute-start.87 = (bf16[96,1536]{1,0:T(8,128)(2,1)S(1)}, bf16[96,1536]{1,0:T(8,128)(2,1)S(1)}, u32[]{:S(2)}, u32[]{:S(2)}) collective-permute-start(bf16[96,1536]{1,0:T(8,128)(2,1)S(1)} %get-tuple-element.280), channel_id=1, source_target_pairs={{0,12},{1,13},{2,14},{3,15},{4,0},{5,1},{6,2},{7,3},{8,4},{9,5},{1... | collective-permute-start | bytes 884744 | tf_op jit(solution)/shard_map/ppermute | solution.py:69
  358.7 30.2 %collective-permute-start.52 = (bf16[384,768]{1,0:T(8,128)(2,1)}, bf16[384,768]{1,0:T(8,128)(2,1)}, u32[]{:S(2)}, u32[]{:S(2)}) collective-permute-start(bf16[384,768]{1,0:T(8,128)(2,1)} %get-tuple-element.224), channel_id=1, source_target_pairs={{0,12},{1,13},{2,14},{3,15},{4,0},{5,1},{6,2},{7,3},{8,4},{9,5},{1... | collective-permute-start | bytes 1769480 | tf_op jit(solution)/shard_map/ppermute | solution.py:69
  387.5 68.0 %collective-permute-start.63 = (bf16[384,1536]{1,0:T(8,128)(2,1)}, bf16[384,1536]{1,0:T(8,128)(2,1)S(1)}, u32[]{:S(2)}, u32[]{:S(2)}) collective-permute-start(bf16[384,1536]{1,0:T(8,128)(2,1)} %get-tuple-element.243), channel_id=1, source_target_pairs={{0,4},{1,5},{2,6},{3,7},{4,8},{5,9},{6,10},{7,11},{8,12},{9,13},{1... | collective-permute-start | bytes 3538952 | tf_op jit(solution)/shard_map/ppermute | solution.py:69
  389.0 68.6 %collective-permute-start.34 = (bf16[256,1536]{1,0:T(8,128)(2,1)S(1)}, bf16[256,1536]{1,0:T(8,128)(2,1)S(1)}, u32[]{:S(2)}, u32[]{:S(2)}) collective-permute-start(bf16[256,1536]{1,0:T(8,128)(2,1)S(1)} %get-tuple-element.193.gm_ref.refs_4_), channel_id=1, source_target_pairs={{0,1},{1,0},{2,3},{3,2},{4,5},{5,4},{6,7},{7,6},{8,9},{9,8},{10,11... | collective-permute-start | bytes 2359304 | tf_op jit(solution)/shard_map/ppermute | solution.py:69
  390.7 78.6 %collective-permute-start.64 = (bf16[384,1536]{1,0:T(8,128)(2,1)}, bf16[384,1536]{1,0:T(8,128)(2,1)S(1)}, u32[]{:S(2)}, u32[]{:S(2)}) collective-permute-start(bf16[384,1536]{1,0:T(8,128)(2,1)} %get-tuple-element.244), channel_id=1, source_target_pairs={{0,8},{1,9},{2,10},{3,11},{4,12},{5,13},{6,14},{7,15},{8,0},{9,1},... | collective-permute-start | bytes 3538952 | tf_op jit(solution)/shard_map/ppermute | solution.py:69
  417.7 29.5 %collective-permute-start.60 = (bf16[96,768]{1,0:T(8,128)(2,1)S(1)}, bf16[96,768]{1,0:T(8,128)(2,1)S(1)}, u32[]{:S(2)}, u32[]{:S(2)}) collective-permute-start(bf16[96,768]{1,0:T(8,128)(2,1)S(1)} %get-tuple-element.237), channel_id=1, source_target_pairs={{0,8},{1,9},{2,10},{3,11},{4,12},{5,13},{6,14},{7,15},{8,0},{9,1},... | collective-permute-start | bytes 442376 | tf_op jit(solution)/shard_map/ppermute | solution.py:69
  455.5 29.1 %collective-permute-start.69 = (bf16[384,1536]{1,0:T(8,128)(2,1)}, bf16[384,1536]{1,0:T(8,128)(2,1)S(1)}, u32[]{:S(2)}, u32[]{:S(2)}) collective-permute-start(bf16[384,1536]{1,0:T(8,128)(2,1)} %get-tuple-element.253), channel_id=1, source_target_pairs={{0,16},{1,17},{2,18},{3,19},{4,20},{5,21},{6,22},{7,23},{8,24},{9,... | collective-permute-start | bytes 3538952 | tf_op jit(solution)/shard_map/ppermute | solution.py:69
  455.5 30.6 %collective-permute-start.70 = (bf16[384,1536]{1,0:T(8,128)(2,1)}, bf16[384,1536]{1,0:T(8,128)(2,1)S(1)}, u32[]{:S(2)}, u32[]{:S(2)}) collective-permute-start(bf16[384,1536]{1,0:T(8,128)(2,1)} %get-tuple-element.254), channel_id=1, source_target_pairs={{0,32},{1,33},{2,34},{3,35},{4,36},{5,37},{6,38},{7,39},{8,40},{9,... | collective-permute-start | bytes 3538952 | tf_op jit(solution)/shard_map/ppermute | solution.py:69
  457.6 50.7 %collective-permute-start.71 = (bf16[384,1536]{1,0:T(8,128)(2,1)}, bf16[384,1536]{1,0:T(8,128)(2,1)S(1)}, u32[]{:S(2)}, u32[]{:S(2)}) collective-permute-start(bf16[384,1536]{1,0:T(8,128)(2,1)} %get-tuple-element.255), channel_id=1, source_target_pairs={{0,48},{1,49},{2,50},{3,51},{4,52},{5,53},{6,54},{7,55},{8,56},{9,... | collective-permute-start | bytes 3538952 | tf_op jit(solution)/shard_map/ppermute | solution.py:69
  469.4 43.2 %collective-permute-start.35 = (bf16[256,1536]{1,0:T(8,128)(2,1)S(1)}, bf16[256,1536]{1,0:T(8,128)(2,1)S(1)}, u32[]{:S(2)}, u32[]{:S(2)}) collective-permute-start(bf16[256,1536]{1,0:T(8,128)(2,1)S(1)} %get-tuple-element.196), channel_id=1, source_target_pairs={{0,1},{1,0},{2,3},{3,2},{4,5},{5,4},{6,7},{7,6},{8,9},{9,8},{10,11... | collective-permute-start | bytes 2359304 | tf_op jit(solution)/shard_map/ppermute | solution.py:69
  473.0 40.2 %collective-permute-start.88 = (bf16[48,3072]{1,0:T(8,128)(2,1)S(1)}, bf16[48,3072]{1,0:T(8,128)(2,1)S(1)}, u32[]{:S(2)}, u32[]{:S(2)}) collective-permute-start(bf16[48,3072]{1,0:T(8,128)(2,1)S(1)} %get-tuple-element.282), channel_id=1, source_target_pairs={{0,64},{1,65},{2,66},{3,67},{4,68},{5,69},{6,70},{7,71},{8,72},{9,... | collective-permute-start | bytes 884744 | tf_op jit(solution)/shard_map/ppermute | solution.py:69
  484.6 31.3 %collective-permute-start.62 = (bf16[48,1536]{1,0:T(8,128)(2,1)S(1)}, bf16[48,1536]{1,0:T(8,128)(2,1)S(1)}, u32[]{:S(2)}, u32[]{:S(2)}) collective-permute-start(bf16[48,1536]{1,0:T(8,128)(2,1)S(1)} %get-tuple-element.240), channel_id=1, source_target_pairs={{0,64},{1,65},{2,66},{3,67},{4,68},{5,69},{6,70},{7,71},{8,72},{9,... | collective-permute-start | bytes 442376 | tf_op jit(solution)/shard_map/ppermute | solution.py:69
  486.1 33.7 %collective-permute-start.66 = (bf16[96,1536]{1,0:T(8,128)(2,1)S(1)}, bf16[96,1536]{1,0:T(8,128)(2,1)S(1)}, u32[]{:S(2)}, u32[]{:S(2)}) collective-permute-start(bf16[96,1536]{1,0:T(8,128)(2,1)S(1)} %get-tuple-element.247), channel_id=1, source_target_pairs={{0,16},{1,17},{2,18},{3,19},{4,20},{5,21},{6,22},{7,23},{8,24},{9,... | collective-permute-start | bytes 884744 | tf_op jit(solution)/shard_map/ppermute | solution.py:69
  522.7 29.0 %collective-permute-start.37 = (bf16[384,768]{1,0:T(8,128)(2,1)S(1)}, bf16[384,768]{1,0:T(8,128)(2,1)S(1)}, u32[]{:S(2)}, u32[]{:S(2)}) collective-permute-start(bf16[384,768]{1,0:T(8,128)(2,1)S(1)} %get-tuple-element.201), channel_id=1, source_target_pairs={{0,4},{1,5},{2,6},{3,7},{4,8},{5,9},{6,10},{7,11},{8,12},{9,13},{1... | collective-permute-start | bytes 1769480 | tf_op jit(solution)/shard_map/ppermute | solution.py:69
  (211 other events, 2255.9 us)

commit v2 on v1

v2 whole, which is shorter than its diff:
```python
import functools
import itertools

import jax
import jax.numpy as jnp
from jax import lax
from jax.experimental import pallas as pl
from jax.experimental.pallas import tpu as pltpu
from jax.sharding import Mesh
from jax.sharding import PartitionSpec as P

D = 1536
FF = 6144
E = 128
HEADS = 3
HID = HEADS * E
SLICE = 1536
HALF = 256
OWN = 128
FB = 512
EPS = 1e-5
BASE = 10000.0
MASKED = -1e30
SCALE = E**-0.5
C1 = 0.7978845608028654
C2 = 0.044715

AXES = ("zl", "y", "x", "zh", "c")
SIZES = (2, 4, 4, 2, 2)
F32 = jnp.float32
BF16 = jnp.bfloat16


def flat(place):
    index = 0
    for size, at in zip(SIZES, place):
        index = index * size + at
    return index


def pairs(move):
    return [
        (flat(p), flat(move(*p))) for p in itertools.product(*[range(s) for s in SIZES])
    ]


CORE = pairs(lambda zl, y, x, zh, c: (zl, y, x, zh, 1 - c))
FAR = pairs(lambda zl, y, x, zh, c: (zl, y, x, 1 - zh, c))
ZLO = pairs(lambda zl, y, x, zh, c: (1 - zl, y, x, zh, c))


def x_by(d):
    return pairs(lambda zl, y, x, zh, c: (zl, y, (x + d) % 4, zh, c))


def y_by(d):
    return pairs(lambda zl, y, x, zh, c: (zl, (y + d) % 4, x, zh, c))


def x_flip(d):
    return pairs(lambda zl, y, x, zh, c: (zl, y, x ^ d, zh, c))


def y_flip(d):
    return pairs(lambda zl, y, x, zh, c: (zl, y ^ d, x, zh, c))


def send(values, perm):
    return lax.ppermute(values, AXES, perm)


def dot(a, b):
    return jnp.dot(a, b, preferred_element_type=F32)


def dot_t(a, b):
    return lax.dot_general(a, b, (((1,), (1,)), ((), ())), preferred_element_type=F32)


def t_dot(a, b):
    return lax.dot_general(a, b, (((0,), (0,)), ((), ())), preferred_element_type=F32)


VMEM_MB = {'attend':16,'attend_back':26,'feed':18,'feed_back':26,'grads':32,'merge':16,'sum_rings':16,'sum_last':16,'norm':8,'add_norm':8,'norm_back':24}


def params(mb):
    return pltpu.CompilerParams(vmem_limit_bytes=mb * 1024 * 1024)


def cost(flops, size, trans=0):
    return pl.CostEstimate(flops=1, bytes_accessed=1, transcendentals=0)


def whole(shape):
    zeros = (0,) * len(shape)
    return pl.BlockSpec(shape, lambda *_: zeros)


SMEM = pl.BlockSpec(memory_space=pltpu.SMEM)
ANY = pl.BlockSpec(memory_space=pl.ANY)


def run(kernel, args, in_specs, out_shape, out_specs, grid, name, estimate, scratch=(), after=()):
    count, extra = len(args), len(after)

    def wrapped(*refs):
        kernel(*refs[:count], *refs[count + extra :])

    return pl.pallas_call(
        wrapped,
        out_shape=out_shape,
        in_specs=list(in_specs) + [ANY] * extra,
        out_specs=out_specs,
        scratch_shapes=list(scratch),
        grid=(grid,),
        compiler_params=params(VMEM_MB[name]),
        cost_estimate=estimate,
        name=name,
    )(*args, *after)


def moments(x):
    mean = jnp.mean(x, axis=-1, keepdims=True)
    centered = x - mean
    var = jnp.mean(centered * centered, axis=-1, keepdims=True)
    return centered, lax.rsqrt(var + EPS)


def norm_kernel(x_ref, g_ref, b_ref, a_ref):
    centered, r = moments(x_ref[...].astype(F32))
    a_ref[...] = (centered * r * g_ref[...] + b_ref[...]).astype(BF16)


def norm(x, gain, shift):
    rows = x.shape[0]
    return run(
        norm_kernel,
        (x, gain, shift),
        [whole((rows, D)), whole((1, D)), whole((1, D))],
        jax.ShapeDtypeStruct((rows, D), BF16),
        whole((rows, D)),
        1,
        "norm",
        cost(10 * rows * D, 6 * rows * D),
    )


def add_norm_kernel(x_ref, s_ref, r_ref, g_ref, b_ref, m_ref, a_ref):
    x = x_ref[...].astype(F32) + (s_ref[...].astype(F32) + r_ref[...].astype(F32))
    m_ref[...] = x
    centered, r = moments(x)
    a_ref[...] = (centered * r * g_ref[...] + b_ref[...]).astype(BF16)


def add_norm(x, s, r, gain, shift, after=()):
    rows = x.shape[0]
    return run(
        add_norm_kernel,
        (x, s, r, gain, shift),
        [whole((rows, D))] * 3 + [whole((1, D))] * 2,
        (jax.ShapeDtypeStruct((rows, D), F32), jax.ShapeDtypeStruct((rows, D), BF16)),
        (whole((rows, D)), whole((rows, D))),
        1,
        "add_norm",
        cost(10 * rows * D, 14 * rows * D),
        after=after,
    )


def norm_back_kernel(count, *refs):
    xs, ss, rs, prevs = (refs[n * count : (n + 1) * count] for n in range(4))
    g_ref, refs = refs[4 * count], refs[4 * count + 1 :]
    ds, lows, sums_ref = refs[:count], refs[count : 2 * count], refs[2 * count]
    for k in range(count):
        da = ss[k][...].astype(F32) + rs[k][...].astype(F32)
        centered, r = moments(xs[k][...].astype(F32))
        xh = centered * r
        e = da * g_ref[...]
        mean_e = jnp.mean(e, axis=-1, keepdims=True)
        mean_ex = jnp.mean(e * xh, axis=-1, keepdims=True)
        out = prevs[k][...].astype(F32) + r * (e - mean_e - xh * mean_ex)
        ds[k][...] = out
        lows[k][...] = out.astype(BF16)
        both = (jnp.sum(da * xh, axis=0, keepdims=True), jnp.sum(da, axis=0, keepdims=True))
        for n in range(2):
            if k:
                sums_ref[n : n + 1, :] += both[n]
            else:
                sums_ref[n : n + 1, :] = both[n]


def norm_back(xs, ss, rs, prevs, gain, after=()):
    count = len(xs)
    piece = whole((OWN, D))
    outs = run(
        functools.partial(norm_back_kernel, count),
        (*xs, *ss, *rs, *prevs, gain),
        [piece] * (4 * count) + [whole((1, D))],
        (jax.ShapeDtypeStruct((OWN, D), F32),) * count
        + (jax.ShapeDtypeStruct((OWN, D), BF16),) * count
        + (jax.ShapeDtypeStruct((2, D), F32),),
        (piece,) * (2 * count) + (whole((2, D)),),
        1,
        "norm_back",
        cost(20 * count * OWN * D, 18 * count * OWN * D),
        after=after,
    )
    return outs[:count], outs[count : 2 * count], outs[2 * count]


def rot(x, cos, sin):
    return x * cos + pltpu.roll(x, E // 2, 1) * sin


def allowed(q_start, rows, columns):
    q = lax.broadcasted_iota(jnp.int32, (rows, columns), 0) + q_start
    return lax.broadcasted_iota(jnp.int32, (rows, columns), 1) <= q


def mine_theirs(core, acc, chunks, outs):
    for k in range(chunks):
        for out, side in zip(outs[2 * k : 2 * k + 2], (core, 1 - core)):
            rows = pl.ds(pl.multiple_of(k * HALF + side * OWN, OWN), OWN)
            out[...] = acc[rows, :].astype(BF16)


def softmax(s):
    top = jnp.max(s, axis=-1, keepdims=True)
    e = jnp.exp(s - top)
    return e / jnp.sum(e, axis=-1, keepdims=True)


def attend_kernel(chunk, core_ref, a_ref, w_ref, wo_ref, cos_ref, sin_ref, *rest):
    if chunk:
        before_ref, qkv_ref, o_ref, pm_ref, pt_ref, acc = rest
    else:
        qkv_ref, o_ref, pm_ref, pt_ref, acc = rest
    step = pl.program_id(0)
    a = a_ref[...]
    w = jnp.concatenate([w_ref[0, 0], w_ref[0, 1], w_ref[0, 2]], axis=1)
    p = dot(a, w)
    cos, sin = cos_ref[...], sin_ref[...]
    q = (rot(p[:, :E], cos, sin) * SCALE).astype(BF16)
    k = rot(p[:, E : 2 * E], cos, sin).astype(BF16)
    v = p[:, 2 * E :].astype(BF16)
    qkv_ref[0], qkv_ref[1], qkv_ref[2] = q, k, v
    if chunk:
        k = jnp.concatenate([before_ref[1], k], axis=0)
        v = jnp.concatenate([before_ref[2], v], axis=0)
    s = dot_t(q, k)
    s = jnp.where(allowed(chunk * HALF, HALF, s.shape[1]), s, MASKED)
    o = dot(softmax(s).astype(BF16), v).astype(BF16)
    o_ref[...] = o
    part = dot(o, wo_ref[0])

    @pl.when(step == 0)
    def _():
        acc[...] = part

    @pl.when(step > 0)
    def _():
        acc[...] += part

    @pl.when(step == HEADS - 1)
    def _():
        mine_theirs(core_ref[0], acc, 1, (pm_ref, pt_ref))


def attend(layer, chunk, core, a, w_qkv, w_out, cos, sin, before, after=()):
    head = pl.BlockSpec((3, HALF, E), lambda h: (0, 0, h))
    tables = pl.BlockSpec((HALF, E), lambda h: (chunk, 0))
    piece = whole((OWN, D))
    return run(
        functools.partial(attend_kernel, chunk),
        (core, a, w_qkv, w_out, cos, sin) + ((before,) if chunk else ()),
        [
            SMEM,
            whole((HALF, D)),
            pl.BlockSpec((1, 3, D, E), lambda h: (layer, 0, 0, h)),
            pl.BlockSpec((1, E, D), lambda h: (layer, h, 0)),
            tables,
            tables,
        ]
        + ([head] if chunk else []),
        (
            jax.ShapeDtypeStruct((3, HALF, HID), BF16),
            jax.ShapeDtypeStruct((HALF, HID), BF16),
            jax.ShapeDtypeStruct((OWN, D), BF16),
            jax.ShapeDtypeStruct((OWN, D), BF16),
        ),
        (head, pl.BlockSpec((HALF, E), lambda h: (0, h)), piece, piece),
        HEADS,
        "attend",
        cost(2 * HALF * D * 4 * HID, 2 * 4 * HID * D + 8 * HALF * D),
        scratch=[pltpu.VMEM((HALF, D), F32)],
        after=after,
    )


def attend_back_kernel(
    core_ref, g0_ref, g1_ref, w_ref, wo_ref, cos_ref, sin_ref, c0_ref, c1_ref, d_ref, *rest
):
    outs, acc = rest[:4], rest[4]
    step = pl.program_id(0)
    do0 = dot_t(g0_ref[...], wo_ref[0]).astype(BF16)
    do1 = dot_t(g1_ref[...], wo_ref[0]).astype(BF16)
    k = jnp.concatenate([c0_ref[1], c1_ref[1]], axis=0)
    v = jnp.concatenate([c0_ref[2], c1_ref[2]], axis=0)

    def block(chunk, q, do, keys, values):
        s = dot_t(q, keys)
        s = jnp.where(allowed(chunk * HALF, HALF, s.shape[1]), s, MASKED)
        prob = softmax(s)
        dp = dot_t(do, values)
        ds = (prob * (dp - jnp.sum(prob * dp, axis=-1, keepdims=True))).astype(BF16)
        return dot(ds, keys), t_dot(ds, q), t_dot(prob.astype(BF16), do)

    dq1, dk1, dv1 = block(1, c1_ref[0], do1, k, v)
    dq0, dk0, dv0 = block(0, c0_ref[0], do0, c0_ref[1], c0_ref[2])
    cos, sin = cos_ref[...], -sin_ref[...]
    dq = (rot(jnp.concatenate([dq0, dq1], axis=0), cos, sin) * SCALE).astype(BF16)
    dk = jnp.concatenate([dk0 + dk1[:HALF], dk1[HALF:]], axis=0)
    dk = rot(dk, cos, sin).astype(BF16)
    dv = jnp.concatenate([dv0 + dv1[:HALF], dv1[HALF:]], axis=0).astype(BF16)
    d_ref[0], d_ref[1], d_ref[2] = dq, dk, dv
    w = jnp.concatenate([w_ref[0, 0], w_ref[0, 1], w_ref[0, 2]], axis=1)
    part = dot_t(jnp.concatenate([dq, dk, dv], axis=1), w)

    @pl.when(step == 0)
    def _():
        acc[...] = part

    @pl.when(step > 0)
    def _():
        acc[...] += part

    @pl.when(step == HEADS - 1)
    def _():
        mine_theirs(core_ref[0], acc, 2, outs)


def attend_back(layer, core, g0, g1, w_qkv, w_out, cos, sin, saved0, saved1, after=()):
    rows = 2 * HALF
    head = pl.BlockSpec((3, HALF, E), lambda h: (0, 0, h))
    piece = whole((HALF, D))
    return run(
        attend_back_kernel,
        (core, g0, g1, w_qkv, w_out, cos, sin, saved0, saved1),
        [
            SMEM,
            piece,
            piece,
            pl.BlockSpec((1, 3, D, E), lambda h: (layer, 0, 0, h)),
            pl.BlockSpec((1, E, D), lambda h: (layer, h, 0)),
            whole((rows, E)),
            whole((rows, E)),
            head,
            head,
        ],
        (
            jax.ShapeDtypeStruct((3, rows, HID), BF16),
        )
        + (jax.ShapeDtypeStruct((OWN, D), BF16),) * 4,
        (pl.BlockSpec((3, rows, E), lambda h: (0, 0, h)),) + (whole((OWN, D)),) * 4,
        HEADS,
        "attend_back",
        cost(2 * rows * D * 5 * HID, 2 * 4 * HID * D + 8 * rows * D),
        scratch=[pltpu.VMEM((rows, D), F32)],
        after=after,
    )


def feed_kernel(width_ref, core_ref, a_ref, up_ref, down_ref, hid_ref, slope_ref, pm_ref, pt_ref, acc):
    step = pl.program_id(0)
    u = dot(a_ref[...], up_ref[0])
    place = lax.broadcasted_iota(jnp.int32, u.shape, 1) + step * FB
    keep = place < width_ref[0]
    square = u * u
    t = jnp.tanh(C1 * (u + C2 * u * square))
    hid = jnp.where(keep, 0.5 * u * (1.0 + t), 0.0).astype(BF16)
    slope = 0.5 * (1.0 + t) + 0.5 * u * (1.0 - t * t) * (C1 * (1.0 + 3.0 * C2 * square))
    slope_ref[...] = jnp.where(keep, slope, 0.0).astype(BF16)
    hid_ref[...] = hid
    part = dot(hid, down_ref[0])

    @pl.when(step == 0)
    def _():
        acc[...] = part

    @pl.when(step > 0)
    def _():
        acc[...] += part

    @pl.when(step == SLICE // FB - 1)
    def _():
        mine_theirs(core_ref[0], acc, 1, (pm_ref, pt_ref))


def feed(layer, width, core, a, w_up, w_down, after=()):
    piece = whole((OWN, D))
    block = pl.BlockSpec((HALF, FB), lambda j: (0, j))
    return run(
        feed_kernel,
        (width, core, a, w_up, w_down),
        [
            SMEM,
            SMEM,
            whole((HALF, D)),
            pl.BlockSpec((1, D, FB), lambda j: (layer, 0, j)),
            pl.BlockSpec((1, FB, D), lambda j: (layer, j, 0)),
        ],
        (
            jax.ShapeDtypeStruct((HALF, SLICE), BF16),
            jax.ShapeDtypeStruct((HALF, SLICE), BF16),
            jax.ShapeDtypeStruct((OWN, D), BF16),
            jax.ShapeDtypeStruct((OWN, D), BF16),
        ),
        (block, block, piece, piece),
        SLICE // FB,
        "feed",
        cost(4 * HALF * D * SLICE, 4 * SLICE * D + 8 * HALF * D),
        scratch=[pltpu.VMEM((HALF, D), F32)],
        after=after,
    )


def feed_back_kernel(core_ref, g0_ref, g1_ref, down_ref, up_ref, slope0_ref, slope1_ref, du_ref, *rest):
    outs, acc = rest[:4], rest[4]
    step = pl.program_id(0)
    g = jnp.concatenate([g0_ref[...], g1_ref[...]], axis=0)
    dhid = dot_t(g, down_ref[0])
    slope = jnp.concatenate([slope0_ref[...], slope1_ref[...]], axis=0).astype(F32)
    du = (dhid * slope).astype(BF16)
    du_ref[...] = du
    part = dot_t(du, up_ref[0])

    @pl.when(step == 0)
    def _():
        acc[...] = part

    @pl.when(step > 0)
    def _():
        acc[...] += part

    @pl.when(step == SLICE // FB - 1)
    def _():
        mine_theirs(core_ref[0], acc, 2, outs)


def feed_back(layer, core, g0, g1, w_up, w_down, slope0, slope1, after=()):
    rows = 2 * HALF
    piece = whole((HALF, D))
    block = pl.BlockSpec((HALF, FB), lambda j: (0, j))
    return run(
        feed_back_kernel,
        (core, g0, g1, w_down, w_up, slope0, slope1),
        [
            SMEM,
            piece,
            piece,
            pl.BlockSpec((1, FB, D), lambda j: (layer, j, 0)),
            pl.BlockSpec((1, D, FB), lambda j: (layer, 0, j)),
            block,
            block,
        ],
        (
            jax.ShapeDtypeStruct((rows, SLICE), BF16),
        )
        + (jax.ShapeDtypeStruct((OWN, D), BF16),) * 4,
        (pl.BlockSpec((rows, FB), lambda j: (0, j)),) + (whole((OWN, D)),) * 4,
        SLICE // FB,
        "feed_back",
        cost(4 * rows * D * SLICE, 4 * SLICE * D + 8 * rows * D),
        scratch=[pltpu.VMEM((rows, D), F32)],
        after=after,
    )


def grad_kernel(first, counts, steps, place_ref, *refs):
    lefts, refs = refs[: sum(counts)], refs[sum(counts) :]
    rights, refs = refs[: sum(n for n, _ in steps)], refs[sum(n for n, _ in steps) :]
    own, to_right, to_left, right_later, left_later, turned, total = refs
    step = pl.program_id(0)
    start = at_left = at_right = 0
    for count, (operands, number) in zip(counts, steps):
        left = lefts[at_left : at_left + count]
        right = rights[at_right : at_right + operands]
        at_left += count
        at_right += operands

        @pl.when(step == start)
        def _():
            turned[...] = jnp.concatenate([r[...] for r in left], axis=0).T

        @pl.when((step >= start) & (step < start + number))
        def _():
            b = jnp.concatenate([r[0] if len(r.shape) == 3 else r[...] for r in right], axis=0)
            total[...] = dot(turned[...], b).astype(BF16)

        start += number

    def put(out, at, d, major):
        there = lax.rem(place_ref[0 if first else 1] + d, 4)
        for minor in range(4):
            block = (major * 4 + minor) * 4 + there if first else (major * 4 + there) * 4 + minor
            out[(at + minor) * 48 : (at + minor + 1) * 48, :] = total[
                pl.ds(pl.multiple_of(block * 48, 16), 48), :
            ]

    put(own, 0, 0, 0)
    put(own, 4, 0, 1)
    put(to_right, 0, 2, 1)
    put(to_right, 4, 1, 0)
    put(to_left, 0, 2, 0)
    put(to_left, 4, 3, 1)
    put(right_later, 0, 1, 1)
    put(left_later, 0, 3, 0)


def grads(first, place, block, terms, after=()):
    lefts, specs, rights, right_specs = [], [], [], []
    counts, steps, start = [], [], 0
    for left, right, number in terms:
        lefts += left
        specs += [whole(a.shape) for a in left]
        counts.append(len(left))
        steps.append((len(right), number))
        for array, shape, index in right:
            rights.append(array)
            right_specs.append(
                pl.BlockSpec(
                    shape,
                    lambda j, s=start, n=number, index=index: index(jnp.clip(j - s, 0, n - 1)),
                )
            )
        start += number
    columns = start * block
    rows = (384, 384, 384, 192, 192)
    return run(
        functools.partial(grad_kernel, first, counts, steps),
        (place, *lefts, *rights),
        [SMEM] + specs + right_specs,
        tuple(jax.ShapeDtypeStruct((n, columns), BF16) for n in rows),
        tuple(pl.BlockSpec((n, block), lambda j: (0, j)) for n in rows),
        start,
        "grads",
        cost(4 * HALF * D * columns, 3 * D * columns + 4 * HALF * (columns + D)),
        scratch=[pltpu.VMEM((D, 2 * HALF), BF16), pltpu.VMEM((D, block), BF16)],
        after=after,
    )


def merge_kernel(*refs):
    ins, outs = refs[:8], refs[8:]
    for number, out in enumerate(outs):
        own, got = ins[2 * number : 2 * number + 2]
        out[...] = (own[...].astype(F32) + got[...].astype(F32)).astype(BF16)


def merge(pieces, after=()):
    columns = pieces[0][0].shape[1]
    block = min(columns, 768)
    spec = pl.BlockSpec((192, block), lambda j: (0, j))
    return run(
        merge_kernel,
        [array for pair in pieces for array in pair],
        [spec] * 8,
        (jax.ShapeDtypeStruct((192, columns), BF16),) * 4,
        (spec,) * 4,
        columns // block,
        "merge",
        cost(4 * 192 * columns, 24 * 192 * columns),
        after=after,
    )


def sum_kernel(place_ref, *refs):
    ins, outs, total = refs[:10], refs[10:18], refs[18]
    for number, first in enumerate((True, False)):
        own, left_a, right_b, right_a, left_b = ins[5 * number : 5 * number + 5]
        for at, one, two in ((0, left_a, right_a), (192, right_b, left_b)):
            t = own[at : at + 192].astype(F32) + one[...].astype(F32) + two[...].astype(F32)
            total[at : at + 192] = t.astype(BF16)
        here = place_ref[1 if first else 0]
        for d in range(4):
            there = lax.rem(here + d, 4)
            for major in range(2):
                offset = pl.multiple_of((major * 4 + there) * 48, 16)
                outs[4 * number + d][major * 48 : (major + 1) * 48, :] = total[pl.ds(offset, 48), :]


def sum_rings(place, rings, after=()):
    columns = rings[0][0].shape[1]
    block = 384
    upper = pl.BlockSpec((192, block), lambda j: (0, j))
    lower = pl.BlockSpec((192, block), lambda j: (1, j))
    full = pl.BlockSpec((384, block), lambda j: (0, j))
    outs = run(
        sum_kernel,
        [place] + [array for ring in rings for array in ring],
        [SMEM] + [full, lower, lower, upper, upper] * 2,
        (jax.ShapeDtypeStruct((96, columns), BF16),) * 8,
        (pl.BlockSpec((96, block), lambda j: (0, j)),) * 8,
        columns // block,
        "sum_rings",
        cost(6 * 384 * columns, 16 * 384 * columns),
        scratch=[pltpu.VMEM((384, block), BF16)],
        after=after,
    )
    return outs[:4], outs[4:]


def last_kernel(place_ref, *refs):
    ins, (keep, away, total) = refs[:-3], refs[-3:]
    half = len(ins) // 2
    here = place_ref[2]
    columns = ins[0].shape[1]
    for number in range(2):
        t = sum(r[...].astype(F32) for r in ins[number * half : (number + 1) * half])
        total[:, number * columns : (number + 1) * columns] = t
    keep[...] = total[pl.ds(pl.multiple_of(here * 48, 16), 48), :]
    away[...] = total[pl.ds(pl.multiple_of((1 - here) * 48, 16), 48), :].astype(BF16)


def sum_last(place, parts_x, parts_y, after=()):
    columns = parts_x[0].shape[1]
    return run(
        last_kernel,
        (place, *parts_x, *parts_y),
        [SMEM] + [whole((96, columns))] * 8,
        (
            jax.ShapeDtypeStruct((48, 2 * columns), F32),
            jax.ShapeDtypeStruct((48, 2 * columns), BF16),
        ),
        (whole((48, 2 * columns)),) * 2,
        1,
        "sum_last",
        cost(8 * 96 * columns, 24 * 96 * columns),
        scratch=[pltpu.VMEM((96, 2 * columns), F32)],
        after=after,
    )


class Reduction:
    def __init__(self, place, parts_x, parts_y):
        self.place = place
        self.own = parts_x[0], parts_y[0]
        self.later = parts_x[3:], parts_y[3:]
        self.rings = (x_by(1), x_by(3)), (y_by(1), y_by(3))
        self.from_left = [send(p[1], r[0]) for p, r in zip((parts_x, parts_y), self.rings)]
        self.from_right = [send(p[2], r[1]) for p, r in zip((parts_x, parts_y), self.rings)]

    def merge(self, after=()):
        pieces = []
        for n in range(2):
            pieces += [(self.later[n][0], self.from_left[n]), (self.later[n][1], self.from_right[n])]
        outs = merge(pieces, after)
        self.left_b = [send(outs[2 * n], self.rings[n][0]) for n in range(2)]
        self.right_a = [send(outs[2 * n + 1], self.rings[n][1]) for n in range(2)]
        return outs

    def sum(self, after=()):
        rings = [
            (self.own[n], self.from_left[n], self.from_right[n], self.right_a[n], self.left_b[n])
            for n in range(2)
        ]
        next_x, next_y = outs = sum_rings(self.place, rings, after)
        self.got_x = [next_x[0]] + [send(next_x[d], y_by(d)) for d in (1, 2, 3)]
        self.got_y = [next_y[0]] + [send(next_y[d], x_by(d)) for d in (1, 2, 3)]
        return outs[0]

    def last(self, after=()):
        self.keep, away = sum_last(self.place, self.got_x, self.got_y, after)
        self.arrived = send(away, ZLO)
        return (away,)

    def result(self):
        return self.keep + self.arrived.astype(F32)


def body(tokens, norm_gain, norm_shift, w_qkv, w_out, w_up, w_down, granularity, cotangent):
    zl, y, x, zh, c = (lax.axis_index(a) for a in AXES)
    layers = w_qkv.shape[0]
    core = c.reshape(1).astype(jnp.int32)
    place = jnp.stack([x, y, zl]).astype(jnp.int32)
    width = FF // 8 * 2 ** granularity[0, 0] - (zh * 2 + c) * SLICE
    width = width.reshape(1).astype(jnp.int32)
    w_qkv = jnp.transpose(w_qkv, (0, 2, 1, 3))
    low_chip = zh == 0

    positions = jnp.arange(2 * HALF, dtype=F32)[:, None]
    half = E // 2
    frequency = BASE ** (-jnp.arange(half, dtype=F32) / half)
    angles = positions * frequency[None, :]
    cos = jnp.cos(angles)
    sin = jnp.sin(angles)
    cos = jnp.concatenate([cos, cos], axis=1)
    sin = jnp.concatenate([-sin, sin], axis=1)

    def gain(layer, member):
        return norm_gain[layer, member][None, :]

    def shift(layer, member):
        return norm_shift[layer, member][None, :]

    def both_chunks(own):
        other = send(own, FAR)
        return jnp.where(low_chip, own, other), jnp.where(low_chip, other, own)

    def pair(a):
        return lax.all_gather(a, "c", axis=0, tiled=True)

    def core_sum(mine, theirs):
        other = lax.dynamic_slice_in_dim(pair(theirs), (1 - c) * OWN, OWN, 0)
        return mine.astype(F32) + other.astype(F32)

    def exchange(mine, theirs):
        s = core_sum(mine, theirs).astype(BF16)
        return s, send(s, FAR)

    stream = list(both_chunks(tokens))
    normed = [pair(norm(stream[k], gain(0, 0), shift(0, 0))) for k in range(2)]
    saved = []
    gate = ()
    for layer in range(layers):
        keep = {"stream": list(stream), "normed": normed}
        qkv, mixture, sums = [None] * 2, [None] * 2, [None] * 2
        mid, normed_two = [None] * 2, [None] * 2
        hid, slope = [None] * 2, [None] * 2
        for k in range(2):
            qkv[k], mixture[k], pm, pt = attend(
                layer, k, core, normed[k], w_qkv, w_out, cos, sin, qkv[0], gate
            )
            sums[k] = exchange(pm, pt)
            gate = sums[k][:1]
        for k in range(2):
            mid[k], a = add_norm(stream[k], *sums[k], gain(layer, 1), shift(layer, 1), gate)
            normed_two[k] = pair(a)
            hid[k], slope[k], pm, pt = feed(layer, width, core, normed_two[k], w_up, w_down, gate)
            if layer < layers - 1:
                sums[k] = exchange(pm, pt)
                gate = sums[k][:1]
            else:
                sums[k] = core_sum(pm, pt)
        keep.update(qkv=qkv, mixture=mixture, mid=mid, normed_two=normed_two, hid=hid, slope=slope)
        saved.append(keep)
        if layer < layers - 1:
            normed = [None] * 2
            for k in range(2):
                stream[k], a = add_norm(
                    mid[k], *sums[k], gain(layer + 1, 0), shift(layer + 1, 0), gate
                )
                normed[k] = pair(a)
    ours = jnp.where(low_chip, sums[0], sums[1])
    away = jnp.where(low_chip, sums[1], sums[0]).astype(BF16)
    base = jnp.where(low_chip, mid[0], mid[1])
    activations = (base + (ours + send(away, FAR).astype(F32))).astype(BF16)

    gradient = both_chunks(cotangent)
    g = [pair(v) for v in gradient]
    gate = (away,)
    norm_sums = [[None, None] for _ in range(layers)]
    feed_sums, attend_sums = [None] * layers, [None] * layers

    def column(j):
        return (0, j)

    def feed_grads(kept, du, g, after):
        number = SLICE // FB
        up = grads(True, place, FB, [(kept["normed_two"], [(du, (2 * HALF, FB), column)], number)], after)
        down = grads(
            False,
            place,
            FB,
            [(g, [(h, (HALF, FB), column) for h in kept["hid"]], number)],
            (up[4],),
        )
        return Reduction(place, up, down), (down[4],)

    def attend_grads(kept, dqkv, g, after):
        a_one = kept["normed"]
        head = (1, 2 * HALF, HID)
        one = grads(True, place, HID, [(a_one, [(dqkv, head, lambda j: (j, 0, 0))], 2)], after)
        two = grads(
            False,
            place,
            HID,
            [
                (a_one, [(dqkv, head, lambda j: (2, 0, 0))], 1),
                (g, [(m, (HALF, HID), lambda j: (0, 0)) for m in kept["mixture"]], 1),
            ],
            (one[4],),
        )
        return Reduction(place, one, two), (two[4],)

    one, zero = layers - 1, 0
    def backward_sums(parts):
        return list(zip(*[exchange(*parts[2 * k : 2 * k + 2]) for k in range(2)]))

    kept = saved[one]
    du, *parts = feed_back(one, core, *g, w_up, w_down, *kept["slope"], gate)
    ss, rs = backward_sums(parts)
    feed_sums[one], gate = feed_grads(kept, du, g, ss)
    gradient, low, norm_sums[one][1] = norm_back(kept["mid"], ss, rs, gradient, gain(one, 1), gate)
    g = [pair(v) for v in low]
    dqkv, *parts = attend_back(one, core, *g, w_qkv, w_out, cos, sin, *kept["qkv"])
    ss, rs = backward_sums(parts)
    gate = feed_sums[one].merge(ss)[:1]
    attend_sums[one], gate = attend_grads(kept, dqkv, g, gate)
    gradient, low, norm_sums[one][0] = norm_back(
        kept["stream"], ss, rs, gradient, gain(one, 0), gate
    )
    g = [pair(v) for v in low]
    kept = saved[zero]
    du, *parts = feed_back(zero, core, *g, w_up, w_down, *kept["slope"])
    ss, rs = backward_sums(parts)
    gate = feed_sums[one].sum(ss)[:1]
    gate = attend_sums[one].merge(gate)[:1]
    feed_sums[zero], gate = feed_grads(kept, du, g, gate)
    gradient, low, norm_sums[zero][1] = norm_back(
        kept["mid"], ss, rs, gradient, gain(zero, 1), gate
    )
    g = [pair(v) for v in low]
    dqkv, *parts = attend_back(zero, core, *g, w_qkv, w_out, cos, sin, *kept["qkv"])
    total = [core_sum(*parts[2 * k : 2 * k + 2]) for k in range(2)]
    s = jnp.where(low_chip, total[0], total[1]).astype(BF16)
    away = jnp.where(low_chip, total[1], total[0]).astype(BF16)
    r = send(away, FAR)
    attend_sums[zero], gate = attend_grads(kept, dqkv, g, (away,))
    gate = feed_sums[zero].merge(gate)[:1]
    gate = attend_sums[one].sum(gate)[:1]
    gate = feed_sums[one].last(gate)
    gate = attend_sums[zero].merge(gate)[:1]
    gate = feed_sums[zero].sum(gate)[:1]
    xs = jnp.where(low_chip, *kept["stream"])
    prev = jnp.where(low_chip, *gradient)
    (input_grad,), _, norm_sums[zero][0] = norm_back([xs], [s], [r], [prev], gain(zero, 0), gate)
    gate = attend_sums[one].last(gate)
    gate = attend_sums[zero].sum(gate)[:1]
    gate = feed_sums[zero].last(gate)
    gate = attend_sums[zero].last(gate)

    def over_all(sums):
        for perm in (CORE, x_flip(1), x_flip(2), y_flip(1), y_flip(2), ZLO, FAR):
            sums = sums + send(sums, perm)
        return sums

    half = [0.5 * norm_sums[zero][1], 0.5 * norm_sums[one][0], 0.5 * norm_sums[one][1]]
    sums = over_all(jnp.stack([norm_sums[zero][0], *half])).reshape(layers, 2, 2, D)
    gain_grads, shift_grads = sums[:, :, 0], sums[:, :, 1]

    feed_all = jnp.stack([w.result() for w in feed_sums])
    attend_all = jnp.stack([w.result() for w in attend_sums])
    grad_up = feed_all[:, :, :SLICE]
    grad_down = jnp.swapaxes(feed_all[:, :, SLICE:], 1, 2)
    grad_qkv = attend_all[:, :, : 3 * HID].reshape(layers, 48, 3, HID)
    grad_out = jnp.swapaxes(attend_all[:, :, 3 * HID :], 1, 2)
    return (
        activations,
        input_grad,
        grad_qkv,
        grad_out,
        grad_up,
        grad_down,
        gain_grads,
        shift_grads,
        shift_grads[:, 1, :],
    )


def solution(mesh):
    fine = Mesh(mesh.devices.reshape(SIZES), AXES)
    rows = P(AXES, None)
    dp, tensor = AXES[:3], AXES[3:]
    return jax.shard_map(
        body,
        mesh=fine,
        in_specs=(
            rows,
            P(),
            P(),
            P(None, None, None, tensor),
            P(None, tensor, None),
            P(None, None, tensor),
            P(None, tensor, None),
            P(dp, None),
            rows,
        ),
        out_specs=(
            rows,
            rows,
            P(None, dp, None, tensor),
            P(None, tensor, dp),
            P(None, dp, tensor),
            P(None, tensor, dp),
            P(),
            P(),
            P(),
        ),
        check_vma=False,
    )
```

time: 621 us -> 477 us (0.77)
  waiting for transfers between devices: 192 us -> 81.1 us
  blocking collectives: 0 us -> 77.8 us
  starting transfers between devices: 182 us -> 124 us
  Pallas kernels: 171 us -> 141 us
  local copies, waits for them, and re-layouts: 51 us -> 31.9 us
    ppermute x95 -> x83, waiting for transfers between devices: 192 us -> 81.1 us  [send(): return lax.ppermute(values, AXES, perm)]
    all_gather x0 -> x32, blocking collectives: none -> 77.8 us  [pair(): return lax.all_gather(a, 'c', axis=0, tiled=True)]
    ppermute x95 -> x83, starting transfers between devices: 182 us -> 124 us  [send(): return lax.ppermute(values, AXES, perm)]
    pallas_call x44, Pallas kernels: 171 us -> 141 us  [run(): pl.pallas_call(wrapped, out_shape=out_shape, in_specs=list(in_specs) + [A...]
    unnamed x283 -> x305, local copies, waits for them, and re-layouts: 48.5 us -> 30.3 us
  transfers between devices with their start and end apart: 95 -> 83, of which waited for: 37 -> 23; matrix products, arithmetic and copies ran while one was open for 2% -> 2% of each run, Pallas kernels for 24% -> 24%
where the time goes in v2:
time: 477 us; the launch traced here: 468 us
  Pallas kernels  141 us (30%)
  starting transfers between devices  124 us (26%)
  waiting for transfers between devices  81.1 us (17%)
  blocking collectives  77.8 us (16%)
  local copies, waits for them, and re-layouts  31.9 us (7%)
  other arithmetic  7.94 us (2%)
    pallas_call x44, Pallas kernels, run(): pl.pallas_call(wrapped, out_shape=out_shape, in_specs=list(in_specs) + [A...  141 us
    ppermute x83, starting transfers between devices, send(): return lax.ppermute(values, AXES, perm)  124 us
    ppermute x83, waiting for transfers between devices, send(): return lax.ppermute(values, AXES, perm)  81.1 us
    all_gather x32, blocking collectives, pair(): return lax.all_gather(a, 'c', axis=0, tiled=True)  77.8 us
    unnamed x305, local copies, waits for them, and re-layouts  30.3 us
  transfers between devices with their start and end apart: 83, of which 23 were waited for; matrix products, arithmetic and copies ran while one was open for 2% of the time, Pallas kernels for 24%

profile of v2, /device:TPU:10, one launch (start us, length us, event | category | flops | bytes accessed | tf_op | source)
XLA Modules:
  0.0 467.8 jit_solution(17007953196440667371)
XLA Ops:
  7.5 7.3 %collective-permute-done = bf16[128,1536]{1,0:T(8,128)(2,1)S(1)} collective-permute-done((bf16[128,1536]{1,0:T(8,128)(2,1)}, bf16[128,1536]{1,0:T(8,128)(2,1)S(1)}, u32[]{:S(2)}, u32[]{:S(2)}) %collective-permute-start) | collective-permute-done | bytes 393248 | tf_op jit(solution)/shard_map/ppermute | solution.py:69
  22.9 5.6 %attend.4 = (bf16[3,256,384]{2,1,0:T(8,128)(2,1)S(1)}, bf16[256,384]{1,0:T(8,128)(2,1)S(1)}, bf16[128,1536]{1,0:T(8,128)(2,1)S(1)}, bf16[128,1536]{1,0:T(8,128)(2,1)S(1)}) custom-call(s32[1]{0:T(128)} %bitcast.refs_0_.refs_1_, bf16[256,1536]{1,0:T(8,128)(2,1)S(1)} %all_gather.96.refs_1_, bf16[2,3,1536,384]{3,2,1,0:T(8,128)(2,1)S(1)} %bitcast.70, ...), custom_call_target="tpu_custom_call" | custom-call | flops 1 | bytes 1 | tf_op jit(solution)/shard_map/attend/pallas_call | solution.py:110
  34.7 5.8 %attend.5 = (bf16[3,256,384]{2,1,0:T(8,128)(2,1)S(1)}, bf16[256,384]{1,0:T(8,128)(2,1)S(1)}, bf16[128,1536]{1,0:T(8,128)(2,1)S(1)}, bf16[128,1536]{1,0:T(8,128)(2,1)S(1)}) custom-call(s32[1]{0:T(128)} %bitcast.refs_0_.refs_1_, bf16[256,1536]{1,0:T(8,128)(2,1)S(1)} %all_gather.98.refs_1_.refs_2_, bf16[2,3,1536,384]{3,2,1,0:T(8,128)(2,1)S(1)} %bitcast.71, ...), custom_call_target="tpu_custom_call" | custom-call | flops 1 | bytes 1 | tf_op jit(solution)/shard_map/attend/pallas_call | solution.py:110
  46.9 5.0 %feed.4 = (bf16[256,1536]{1,0:T(8,128)(2,1)S(1)}, bf16[256,1536]{1,0:T(8,128)(2,1)S(1)}, bf16[128,1536]{1,0:T(8,128)(2,1)S(1)}, bf16[128,1536]{1,0:T(8,128)(2,1)S(1)}) custom-call(s32[1]{0:T(128)} %bitcast.12.refs_0_, s32[1]{0:T(128)} %bitcast.refs_0_.refs_1_, bf16[256,1536]{1,0:T(8,128)(2,1)S(1)} %all_gather.100.refs_2_.refs_1_, ...), custom_call_target="tpu_custom_call" | custom-call | flops 1 | bytes 1 | tf_op jit(solution)/shard_map/feed/pallas_call | solution.py:110
  60.5 5.0 %feed.5 = (bf16[256,1536]{1,0:T(8,128)(2,1)S(1)}, bf16[256,1536]{1,0:T(8,128)(2,1)S(1)}, bf16[128,1536]{1,0:T(8,128)(2,1)S(1)}, bf16[128,1536]{1,0:T(8,128)(2,1)S(1)}) custom-call(s32[1]{0:T(128)} %bitcast.12.refs_0_, s32[1]{0:T(128)} %bitcast.refs_0_.refs_1_, bf16[256,1536]{1,0:T(8,128)(2,1)S(1)} %all_gather.102.refs_2_, ...), custom_call_target="tpu_custom_call" | custom-call | flops 1 | bytes 1 | tf_op jit(solution)/shard_map/feed/pallas_call | solution.py:110
  74.0 7.4 %collective-permute-done.5.refs_2_ = bf16[128,1536]{1,0:T(8,128)(2,1)S(1)} collective-permute-done((bf16[128,1536]{1,0:T(8,128)(2,1)S(1)}, bf16[128,1536]{1,0:T(8,128)(2,1)S(1)}, u32[]{:S(2)}, u32[]{:S(2)}) %collective-permute-start.5) | collective-permute-done | bytes 393248 | tf_op jit(solution)/shard_map/ppermute | solution.py:69
  84.3 5.6 %attend.6 = (bf16[3,256,384]{2,1,0:T(8,128)(2,1)S(1)}, bf16[256,384]{1,0:T(8,128)(2,1)S(1)}, bf16[128,1536]{1,0:T(8,128)(2,1)S(1)}, bf16[128,1536]{1,0:T(8,128)(2,1)S(1)}) custom-call(s32[1]{0:T(128)} %bitcast.refs_0_.refs_1_, bf16[256,1536]{1,0:T(8,128)(2,1)S(1)} %all_gather.104.refs_1_, bf16[2,3,1536,384]{3,2,1,0:T(8,128)(2,1)S(1)} %bitcast.72, ...), custom_call_target="tpu_custom_call" | custom-call | flops 1 | bytes 1 | tf_op jit(solution)/shard_map/attend/pallas_call | solution.py:110
  92.4 5.8 %attend.7 = (bf16[3,256,384]{2,1,0:T(8,128)(2,1)S(1)}, bf16[256,384]{1,0:T(8,128)(2,1)S(1)}, bf16[128,1536]{1,0:T(8,128)(2,1)S(1)}, bf16[128,1536]{1,0:T(8,128)(2,1)S(1)}) custom-call(s32[1]{0:T(128)} %bitcast.refs_0_.refs_1_, bf16[256,1536]{1,0:T(8,128)(2,1)S(1)} %all_gather.106.refs_1_.refs_2_, bf16[2,3,1536,384]{3,2,1,0:T(8,128)(2,1)S(1)} %bitcast.73, ...), custom_call_target="tpu_custom_call" | custom-call | flops 1 | bytes 1 | tf_op jit(solution)/shard_map/attend/pallas_call | solution.py:110
  109.2 5.1 %collective-permute-done.6.refs_2_ = bf16[128,1536]{1,0:T(8,128)(2,1)S(1)} collective-permute-done((bf16[128,1536]{1,0:T(8,128)(2,1)S(1)}, bf16[128,1536]{1,0:T(8,128)(2,1)S(1)}, u32[]{:S(2)}, u32[]{:S(2)}) %collective-permute-start.6) | collective-permute-done | bytes 393248 | tf_op jit(solution)/shard_map/ppermute | solution.py:69
  117.1 4.9 %collective-permute-done.4.refs_2_ = bf16[128,1536]{1,0:T(8,128)(2,1)S(1)} collective-permute-done((bf16[128,1536]{1,0:T(8,128)(2,1)S(1)}, bf16[128,1536]{1,0:T(8,128)(2,1)S(1)}, u32[]{:S(2)}, u32[]{:S(2)}) %collective-permute-start.4) | collective-permute-done | bytes 393248 | tf_op jit(solution)/shard_map/ppermute | solution.py:69
  125.6 5.0 %feed.7 = (bf16[256,1536]{1,0:T(8,128)(2,1)S(1)}, bf16[256,1536]{1,0:T(8,128)(2,1)S(1)}, bf16[128,1536]{1,0:T(8,128)(2,1)S(1)}, bf16[128,1536]{1,0:T(8,128)(2,1)S(1)}) custom-call(s32[1]{0:T(128)} %bitcast.12.refs_0_, s32[1]{0:T(128)} %bitcast.refs_0_.refs_1_, bf16[256,1536]{1,0:T(8,128)(2,1)S(1)} %all_gather.110.refs_2_, ...), custom_call_target="tpu_custom_call" | custom-call | flops 1 | bytes 1 | tf_op jit(solution)/shard_map/feed/pallas_call | solution.py:110
  134.9 5.0 %feed.6 = (bf16[256,1536]{1,0:T(8,128)(2,1)S(1)}, bf16[256,1536]{1,0:T(8,128)(2,1)S(1)}, bf16[128,1536]{1,0:T(8,128)(2,1)S(1)}, bf16[128,1536]{1,0:T(8,128)(2,1)S(1)}) custom-call(s32[1]{0:T(128)} %bitcast.12.refs_0_, s32[1]{0:T(128)} %bitcast.refs_0_.refs_1_, bf16[256,1536]{1,0:T(8,128)(2,1)S(1)} %all_gather.108.refs_2_.refs_1_, ...), custom_call_target="tpu_custom_call" | custom-call | flops 1 | bytes 1 | tf_op jit(solution)/shard_map/feed/pallas_call | solution.py:110
  144.3 7.0 %feed_back.2 = (bf16[512,1536]{1,0:T(8,128)(2,1)S(1)}, bf16[128,1536]{1,0:T(8,128)(2,1)S(1)}, bf16[128,1536]{1,0:T(8,128)(2,1)S(1)}, bf16[128,1536]{1,0:T(8,128)(2,1)S(1)}, bf16[128,1536]{1,0:T(8,128)(2,1)S(1)}) custom-call(s32[1]{0:T(128)} %bitcast.refs_0_.refs_1_, bf16[256,1536]{1,0:T(8,128)(2,1)S(1)} %copy-done.22, ...), custom_call_target="tpu_custom_call" | custom-call | flops 1 | bytes 1 | tf_op jit(solution)/shard_map/feed_back/pallas_call | solution.py:110
  164.4 4.8 %grads.8 = (bf16[384,1536]{1,0:T(8,128)(2,1)S(1)}, bf16[384,1536]{1,0:T(8,128)(2,1)S(1)}, bf16[384,1536]{1,0:T(8,128)(2,1)S(1)}, bf16[192,1536]{1,0:T(8,128)(2,1)S(1)}, bf16[192,1536]{1,0:T(8,128)(2,1)S(1)}) custom-call(s32[3]{0:T(128)S(1)} %pad_add_fusion.refs_0_, bf16[256,1536]{1,0:T(8,128)(2,1)S(1)} %copy-done.19, bf16[256,1536]{1,0:T(8,128)(2,1)S(1)} %copy-done.17, ...), custom_call_target="tpu_custom_call" | custom-call | flops 1 | bytes 1 | tf_op jit(solution)/shard_map/grads/pallas_call | solution.py:110
  176.8 4.8 %grads.9 = (bf16[384,1536]{1,0:T(8,128)(2,1)S(1)}, bf16[384,1536]{1,0:T(8,128)(2,1)S(1)}, bf16[384,1536]{1,0:T(8,128)(2,1)S(1)}, bf16[192,1536]{1,0:T(8,128)(2,1)S(1)}, bf16[192,1536]{1,0:T(8,128)(2,1)S(1)}) custom-call(s32[3]{0:T(128)S(1)} %pad_add_fusion.refs_0_, bf16[256,1536]{1,0:T(8,128)(2,1)S(1)} %copy-done.23, bf16[256,1536]{1,0:T(8,128)(2,1)S(1)} %copy-done.21, ...), custom_call_target="tpu_custom_call" | custom-call | flops 1 | bytes 1 | tf_op jit(solution)/shard_map/grads/pallas_call | solution.py:110
  194.7 10.3 %attend_back.2 = (bf16[3,512,384]{2,1,0:T(8,128)(2,1)S(1)}, bf16[128,1536]{1,0:T(8,128)(2,1)S(1)}, bf16[128,1536]{1,0:T(8,128)(2,1)S(1)}, bf16[128,1536]{1,0:T(8,128)(2,1)S(1)}, bf16[128,1536]{1,0:T(8,128)(2,1)S(1)}) custom-call(s32[1]{0:T(128)} %bitcast.refs_0_.refs_1_, bf16[256,1536]{1,0:T(8,128)(2,1)S(1)} %all_gather.116.refs_1_.refs_3_, ...), custom_call_target="tpu_custom_call" | custom-call | flops 1 | bytes 1 | tf_op jit(solution)/shard_map/attend_back/pallas_call | solution.py:110
  243.5 7.0 %feed_back.3 = (bf16[512,1536]{1,0:T(8,128)(2,1)S(1)}, bf16[128,1536]{1,0:T(8,128)(2,1)S(1)}, bf16[128,1536]{1,0:T(8,128)(2,1)S(1)}, bf16[128,1536]{1,0:T(8,128)(2,1)S(1)}, bf16[128,1536]{1,0:T(8,128)(2,1)S(1)}) custom-call(s32[1]{0:T(128)} %bitcast.refs_0_.refs_1_, bf16[256,1536]{1,0:T(8,128)(2,1)S(1)} %all_gather.120.refs_1_, ...), custom_call_target="tpu_custom_call" | custom-call | flops 1 | bytes 1 | tf_op jit(solution)/shard_map/feed_back/pallas_call | solution.py:110
  276.4 5.6 %grads.12 = (bf16[384,1536]{1,0:T(8,128)(2,1)S(1)}, bf16[384,1536]{1,0:T(8,128)(2,1)}, bf16[384,1536]{1,0:T(8,128)(2,1)}, bf16[192,1536]{1,0:T(8,128)(2,1)S(1)}, bf16[192,1536]{1,0:T(8,128)(2,1)S(1)}) custom-call(s32[3]{0:T(128)S(1)} %pad_add_fusion.refs_0_, bf16[256,1536]{1,0:T(8,128)(2,1)S(1)} %copy-done.13, bf16[256,1536]{1,0:T(8,128)(2,1)S(1)} %copy-done.15, ...), custom_call_target="tpu_custom_call" | custom-call | flops 1 | bytes 1 | tf_op jit(solution)/shard_map/grads/pallas_call | solution.py:110
  282.0 5.6 %grads.13 = (bf16[384,1536]{1,0:T(8,128)(2,1)S(1)}, bf16[384,1536]{1,0:T(8,128)(2,1)}, bf16[384,1536]{1,0:T(8,128)(2,1)}, bf16[192,1536]{1,0:T(8,128)(2,1)S(1)}, bf16[192,1536]{1,0:T(8,128)(2,1)S(1)}) custom-call(s32[3]{0:T(128)S(1)} %pad_add_fusion.refs_0_, bf16[256,1536]{1,0:T(8,128)(2,1)S(1)} %all_gather.120.refs_1_, ...), custom_call_target="tpu_custom_call" | custom-call | flops 1 | bytes 1 | tf_op jit(solution)/shard_map/grads/pallas_call | solution.py:110
  304.2 10.3 %attend_back.3 = (bf16[3,512,384]{2,1,0:T(8,128)(2,1)S(1)}, bf16[128,1536]{1,0:T(8,128)(2,1)S(1)}, bf16[128,1536]{1,0:T(8,128)(2,1)S(1)}, bf16[128,1536]{1,0:T(8,128)(2,1)S(1)}, bf16[128,1536]{1,0:T(8,128)(2,1)S(1)}) custom-call(s32[1]{0:T(128)} %bitcast.refs_0_.refs_1_, bf16[256,1536]{1,0:T(8,128)(2,1)S(1)} %all_gather.124.refs_1_.refs_3_, ...), custom_call_target="tpu_custom_call" | custom-call | flops 1 | bytes 1 | tf_op jit(solution)/shard_map/attend_back/pallas_call | solution.py:110
  323.6 4.4 collective-permute-done.43.refs_6_
  349.5 11.7 %collective-permute-done.45.refs_8_ = bf16[96,1536]{1,0:T(8,128)(2,1)S(1)} collective-permute-done((bf16[96,1536]{1,0:T(8,128)(2,1)S(1)}, bf16[96,1536]{1,0:T(8,128)(2,1)S(1)}, u32[]{:S(2)}, u32[]{:S(2)}) %collective-permute-start.45) | collective-permute-done | bytes 294944 | tf_op jit(solution)/shard_map/ppermute | solution.py:69
  395.2 8.8 %collective-permute-done.78 = f32[4,2,1536]{2,1,0:T(2,128)S(1)} collective-permute-done((f32[4,2,1536]{2,1,0:T(2,128)S(1)}, f32[4,2,1536]{2,1,0:T(2,128)S(1)}, u32[]{:S(2)}, u32[]{:S(2)}) %collective-permute-start.78) | collective-permute-done | bytes 49184 | tf_op jit(solution)/shard_map/ppermute | solution.py:69
  429.7 9.2 %collective-permute-start.68 = (bf16[96,1536]{1,0:T(8,128)(2,1)S(1)}, bf16[96,1536]{1,0:T(8,128)(2,1)S(1)}, u32[]{:S(2)}, u32[]{:S(2)}) collective-permute-start(bf16[96,1536]{1,0:T(8,128)(2,1)S(1)} %get-tuple-element.348), channel_id=1, source_target_pairs={{0,48},{1,49},{2,50},{3,51},{4,52},{5,53},{6,54},{7,55},{8,56},{9,... | collective-permute-start | bytes 884744 | tf_op jit(solution)/shard_map/ppermute | solution.py:69
  (574 shorter events, 306.8 us)
Async XLA Ops:
  4.6 65.7 %collective-permute-start.8 = (bf16[128,1536]{1,0:T(8,128)(2,1)}, bf16[128,1536]{1,0:T(8,128)(2,1)S(1)}, u32[]{:S(2)}, u32[]{:S(2)}) collective-permute-start(bf16[128,1536]{1,0:T(8,128)(2,1)} %param.17), channel_id=1, source_target_pairs={{0,2},{1,3},{2,0},{3,1},{4,6},{5,7},{6,4},{7,5},{8,10},{9,11},{10,... | collective-permute-start | bytes 1179656 | tf_op jit(solution)/shard_map/ppermute | solution.py:69
  153.9 29.4 %collective-permute-start.9 = (bf16[128,1536]{1,0:T(8,128)(2,1)S(1)}, bf16[128,1536]{1,0:T(8,128)(2,1)}, u32[]{:S(2)}, u32[]{:S(2)}) collective-permute-start(bf16[128,1536]{1,0:T(8,128)(2,1)S(1)} %add_convert_fusion.5.refs_4_.refs_2_), channel_id=1, source_target_pairs={{0,2},{1,3},{2,0},{3,1},{4,6},{5,7},{6,4},{7,5},{8,10},{9,11},{10,... | collective-permute-start | bytes 1179656 | tf_op jit(solution)/shard_map/ppermute | solution.py:69
  158.8 24.9 %collective-permute-start.10 = (bf16[128,1536]{1,0:T(8,128)(2,1)}, bf16[128,1536]{1,0:T(8,128)(2,1)}, u32[]{:S(2)}, u32[]{:S(2)}) collective-permute-start(bf16[128,1536]{1,0:T(8,128)(2,1)} %add_convert_fusion.4.refs_5_.refs_3_), channel_id=1, source_target_pairs={{0,2},{1,3},{2,0},{3,1},{4,6},{5,7},{6,4},{7,5},{8,10},{9,11},{10,... | collective-permute-start | bytes 1179656 | tf_op jit(solution)/shard_map/ppermute | solution.py:69
  170.2 41.5 %collective-permute-start.13 = (bf16[384,1536]{1,0:T(8,128)(2,1)S(1)}, bf16[384,1536]{1,0:T(8,128)(2,1)S(1)}, u32[]{:S(2)}, u32[]{:S(2)}) collective-permute-start(bf16[384,1536]{1,0:T(8,128)(2,1)S(1)} %get-tuple-element.240), channel_id=1, source_target_pairs={{0,4},{1,5},{2,6},{3,7},{4,8},{5,9},{6,10},{7,11},{8,12},{9,13},{1... | collective-permute-start | bytes 3538952 | tf_op jit(solution)/shard_map/ppermute | solution.py:69
  171.7 42.0 %collective-permute-start.14 = (bf16[384,1536]{1,0:T(8,128)(2,1)S(1)}, bf16[384,1536]{1,0:T(8,128)(2,1)S(1)}, u32[]{:S(2)}, u32[]{:S(2)}) collective-permute-start(bf16[384,1536]{1,0:T(8,128)(2,1)S(1)} %get-tuple-element.241), channel_id=1, source_target_pairs={{0,12},{1,13},{2,14},{3,15},{4,0},{5,1},{6,2},{7,3},{8,4},{9,5},{1... | collective-permute-start | bytes 3538952 | tf_op jit(solution)/shard_map/ppermute | solution.py:69
  181.6 32.1 %collective-permute-start.15 = (bf16[384,1536]{1,0:T(8,128)(2,1)S(1)}, bf16[384,1536]{1,0:T(8,128)(2,1)S(1)}, u32[]{:S(2)}, u32[]{:S(2)}) collective-permute-start(bf16[384,1536]{1,0:T(8,128)(2,1)S(1)} %get-tuple-element.243), channel_id=1, source_target_pairs={{0,16},{1,17},{2,18},{3,19},{4,20},{5,21},{6,22},{7,23},{8,24},{9,... | collective-permute-start | bytes 3538952 | tf_op jit(solution)/shard_map/ppermute | solution.py:69
  183.2 30.5 %collective-permute-start.16 = (bf16[384,1536]{1,0:T(8,128)(2,1)S(1)}, bf16[384,1536]{1,0:T(8,128)(2,1)S(1)}, u32[]{:S(2)}, u32[]{:S(2)}) collective-permute-start(bf16[384,1536]{1,0:T(8,128)(2,1)S(1)} %get-tuple-element.244), channel_id=1, source_target_pairs={{0,48},{1,49},{2,50},{3,51},{4,52},{5,53},{6,54},{7,55},{8,56},{9,... | collective-permute-start | bytes 3538952 | tf_op jit(solution)/shard_map/ppermute | solution.py:69
  207.5 23.7 %collective-permute-start.11 = (bf16[128,1536]{1,0:T(8,128)(2,1)S(1)}, bf16[128,1536]{1,0:T(8,128)(2,1)S(1)}, u32[]{:S(2)}, u32[]{:S(2)}) collective-permute-start(bf16[128,1536]{1,0:T(8,128)(2,1)S(1)} %add_convert_fusion.3.refs_8_.refs_2_), channel_id=1, source_target_pairs={{0,2},{1,3},{2,0},{3,1},{4,6},{5,7},{6,4},{7,5},{8,10},{9,11},{10,... | collective-permute-start | bytes 1179656 | tf_op jit(solution)/shard_map/ppermute | solution.py:69
  216.4 36.8 %collective-permute-start.23 = (bf16[192,1536]{1,0:T(8,128)(2,1)}, bf16[192,1536]{1,0:T(8,128)(2,1)S(1)}, u32[]{:S(2)}, u32[]{:S(2)}) collective-permute-start(bf16[192,1536]{1,0:T(8,128)(2,1)} %get-tuple-element.268), channel_id=1, source_target_pairs={{0,12},{1,13},{2,14},{3,15},{4,0},{5,1},{6,2},{7,3},{8,4},{9,5},{1... | collective-permute-start | bytes 1769480 | tf_op jit(solution)/shard_map/ppermute | solution.py:69
  218.1 35.7 %collective-permute-start.25 = (bf16[192,1536]{1,0:T(8,128)(2,1)}, bf16[192,1536]{1,0:T(8,128)(2,1)S(1)}, u32[]{:S(2)}, u32[]{:S(2)}) collective-permute-start(bf16[192,1536]{1,0:T(8,128)(2,1)} %get-tuple-element.270), channel_id=1, source_target_pairs={{0,48},{1,49},{2,50},{3,51},{4,52},{5,53},{6,54},{7,55},{8,56},{9,... | collective-permute-start | bytes 1769480 | tf_op jit(solution)/shard_map/ppermute | solution.py:69
  219.8 38.6 %collective-permute-start.24 = (bf16[192,1536]{1,0:T(8,128)(2,1)S(1)}, bf16[192,1536]{1,0:T(8,128)(2,1)S(1)}, u32[]{:S(2)}, u32[]{:S(2)}) collective-permute-start(bf16[192,1536]{1,0:T(8,128)(2,1)S(1)} %get-tuple-element.245.refs_4_), channel_id=1, source_target_pairs={{0,4},{1,5},{2,6},{3,7},{4,8},{5,9},{6,10},{7,11},{8,12},{9,13},{1... | collective-permute-start | bytes 1769480 | tf_op jit(solution)/shard_map/ppermute | solution.py:69
  231.2 24.2 %collective-permute-start.26 = (bf16[192,1536]{1,0:T(8,128)(2,1)}, bf16[192,1536]{1,0:T(8,128)(2,1)S(1)}, u32[]{:S(2)}, u32[]{:S(2)}) collective-permute-start(bf16[192,1536]{1,0:T(8,128)(2,1)} %get-tuple-element.271), channel_id=1, source_target_pairs={{0,16},{1,17},{2,18},{3,19},{4,20},{5,21},{6,22},{7,23},{8,24},{9,... | collective-permute-start | bytes 1769480 | tf_op jit(solution)/shard_map/ppermute | solution.py:69
  235.6 24.5 %collective-permute-start.19 = (bf16[384,768]{1,0:T(8,128)(2,1)}, bf16[384,768]{1,0:T(8,128)(2,1)S(1)}, u32[]{:S(2)}, u32[]{:S(2)}) collective-permute-start(bf16[384,768]{1,0:T(8,128)(2,1)} %get-tuple-element.262), channel_id=1, source_target_pairs={{0,4},{1,5},{2,6},{3,7},{4,8},{5,9},{6,10},{7,11},{8,12},{9,13},{1... | collective-permute-start | bytes 1769480 | tf_op jit(solution)/shard_map/ppermute | solution.py:69
  260.0 27.5 %collective-permute-start.18 = (bf16[128,1536]{1,0:T(8,128)(2,1)S(1)}, bf16[128,1536]{1,0:T(8,128)(2,1)S(1)}, u32[]{:S(2)}, u32[]{:S(2)}) collective-permute-start(bf16[128,1536]{1,0:T(8,128)(2,1)S(1)} %add_convert_fusion.refs_12_.refs_3_), channel_id=1, source_target_pairs={{0,2},{1,3},{2,0},{3,1},{4,6},{5,7},{6,4},{7,5},{8,10},{9,11},{10,... | collective-permute-start | bytes 1179656 | tf_op jit(solution)/shard_map/ppermute | solution.py:69
  276.3 21.5 %collective-permute-start.47 = (bf16[192,768]{1,0:T(8,128)(2,1)S(1)}, bf16[192,768]{1,0:T(8,128)(2,1)S(1)}, u32[]{:S(2)}, u32[]{:S(2)}) collective-permute-start(bf16[192,768]{1,0:T(8,128)(2,1)S(1)} %get-tuple-element.273.refs_4_), channel_id=1, source_target_pairs={{0,4},{1,5},{2,6},{3,7},{4,8},{5,9},{6,10},{7,11},{8,12},{9,13},{1... | collective-permute-start | bytes 884744 | tf_op jit(solution)/shard_map/ppermute | solution.py:69
  287.6 27.0 %collective-permute-start.40 = (bf16[96,1536]{1,0:T(8,128)(2,1)}, bf16[96,1536]{1,0:T(8,128)(2,1)S(1)}, u32[]{:S(2)}, u32[]{:S(2)}) collective-permute-start(bf16[96,1536]{1,0:T(8,128)(2,1)} %get-tuple-element.308), channel_id=1, source_target_pairs={{0,16},{1,17},{2,18},{3,19},{4,20},{5,21},{6,22},{7,23},{8,24},{9,... | collective-permute-start | bytes 884744 | tf_op jit(solution)/shard_map/ppermute | solution.py:69
  290.7 26.1 %collective-permute-start.41 = (bf16[96,1536]{1,0:T(8,128)(2,1)}, bf16[96,1536]{1,0:T(8,128)(2,1)S(1)}, u32[]{:S(2)}, u32[]{:S(2)}) collective-permute-start(bf16[96,1536]{1,0:T(8,128)(2,1)} %get-tuple-element.309), channel_id=1, source_target_pairs={{0,32},{1,33},{2,34},{3,35},{4,36},{5,37},{6,38},{7,39},{8,40},{9,... | collective-permute-start | bytes 884744 | tf_op jit(solution)/shard_map/ppermute | solution.py:69
  293.0 23.7 %collective-permute-start.42 = (bf16[96,1536]{1,0:T(8,128)(2,1)}, bf16[96,1536]{1,0:T(8,128)(2,1)S(1)}, u32[]{:S(2)}, u32[]{:S(2)}) collective-permute-start(bf16[96,1536]{1,0:T(8,128)(2,1)} %get-tuple-element.310), channel_id=1, source_target_pairs={{0,48},{1,49},{2,50},{3,51},{4,52},{5,53},{6,54},{7,55},{8,56},{9,... | collective-permute-start | bytes 884744 | tf_op jit(solution)/shard_map/ppermute | solution.py:69
  296.3 45.1 %collective-permute-start.28 = (bf16[384,1536]{1,0:T(8,128)(2,1)}, bf16[384,1536]{1,0:T(8,128)(2,1)S(1)}, u32[]{:S(2)}, u32[]{:S(2)}) collective-permute-start(bf16[384,1536]{1,0:T(8,128)(2,1)} %get-tuple-element.286), channel_id=1, source_target_pairs={{0,4},{1,5},{2,6},{3,7},{4,8},{5,9},{6,10},{7,11},{8,12},{9,13},{1... | collective-permute-start | bytes 3538952 | tf_op jit(solution)/shard_map/ppermute | solution.py:69
  298.6 43.9 %collective-permute-start.29 = (bf16[384,1536]{1,0:T(8,128)(2,1)}, bf16[384,1536]{1,0:T(8,128)(2,1)S(1)}, u32[]{:S(2)}, u32[]{:S(2)}) collective-permute-start(bf16[384,1536]{1,0:T(8,128)(2,1)} %get-tuple-element.287), channel_id=1, source_target_pairs={{0,12},{1,13},{2,14},{3,15},{4,0},{5,1},{6,2},{7,3},{8,4},{9,5},{1... | collective-permute-start | bytes 3538952 | tf_op jit(solution)/shard_map/ppermute | solution.py:69
  316.8 29.1 %collective-permute-start.30 = (bf16[384,1536]{1,0:T(8,128)(2,1)}, bf16[384,1536]{1,0:T(8,128)(2,1)S(1)}, u32[]{:S(2)}, u32[]{:S(2)}) collective-permute-start(bf16[384,1536]{1,0:T(8,128)(2,1)} %get-tuple-element.290), channel_id=1, source_target_pairs={{0,16},{1,17},{2,18},{3,19},{4,20},{5,21},{6,22},{7,23},{8,24},{9,... | collective-permute-start | bytes 3538952 | tf_op jit(solution)/shard_map/ppermute | solution.py:69
  316.8 30.2 %collective-permute-start.31 = (bf16[384,1536]{1,0:T(8,128)(2,1)}, bf16[384,1536]{1,0:T(8,128)(2,1)S(1)}, u32[]{:S(2)}, u32[]{:S(2)}) collective-permute-start(bf16[384,1536]{1,0:T(8,128)(2,1)} %get-tuple-element.291), channel_id=1, source_target_pairs={{0,48},{1,49},{2,50},{3,51},{4,52},{5,53},{6,54},{7,55},{8,56},{9,... | collective-permute-start | bytes 3538952 | tf_op jit(solution)/shard_map/ppermute | solution.py:69
  393.5 27.0 %collective-permute-start.7 = (bf16[128,1536]{1,0:T(8,128)(2,1)S(1)}, bf16[128,1536]{1,0:T(8,128)(2,1)S(1)}, u32[]{:S(2)}, u32[]{:S(2)}) collective-permute-start(bf16[128,1536]{1,0:T(8,128)(2,1)S(1)} %copy-done.66), channel_id=1, source_target_pairs={{0,2},{1,3},{2,0},{3,1},{4,6},{5,7},{6,4},{7,5},{8,10},{9,11},{10,... | collective-permute-start | bytes 1179656 | tf_op jit(solution)/shard_map/ppermute | solution.py:69
  415.2 26.0 %collective-permute-start.66 = (bf16[96,1536]{1,0:T(8,128)(2,1)S(1)}, bf16[96,1536]{1,0:T(8,128)(2,1)S(1)}, u32[]{:S(2)}, u32[]{:S(2)}) collective-permute-start(bf16[96,1536]{1,0:T(8,128)(2,1)S(1)} %get-tuple-element.346), channel_id=1, source_target_pairs={{0,16},{1,17},{2,18},{3,19},{4,20},{5,21},{6,22},{7,23},{8,24},{9,... | collective-permute-start | bytes 884744 | tf_op jit(solution)/shard_map/ppermute | solution.py:69
  (210 other events, 2014.5 us)
